TPU v7x, 256 devices: a whole 4x4x8 slice. The times are simulated.
256 devices in a mesh: seq: 32 (over z, y), vocab: 8 (over x, core).
Axes of the slice: x: 4, y: 4, z: 8, core: 2. Of those that a mesh axis runs over, the one named last changes fastest.
Arguments:
- queries: bfloat16 [512, 8192], P('seq'), may hold values from -200 to 200
- span_keys: bfloat16 [512, 1024], P('seq'), may hold values from -3 to 3
- span_head_values: bfloat16 [512, 1024], P('seq'), may hold values from -24 to 24
- prefix_cached_keys: bfloat16 [65536, 1024], P(('seq', 'vocab')), may hold values from -6 to 6
- prefix_cached_values: bfloat16 [65536, 1024], P(('seq', 'vocab')), may hold values from -24 to 24
- start: int32 [1], replicated, may hold values from 32768 to 65536
- out_weight: bfloat16 [8192, 8192], P('seq', 'vocab'), may hold values from -0.25 to 0.25
- residual: bfloat16 [512, 8192], P('seq', 'vocab')
- norm_gain: float32 [8192], P('vocab'), may hold values from 0.5 to 1.5
- head_weight: bfloat16 [8192, 65536], P('vocab', 'seq')
- targets: int32 [512], P('vocab'), may hold values from 0 to 65535
Outputs:
- hidden: bfloat16 [512, 8192], P('seq', 'vocab')
- logprobs: float32 [512], P('vocab')
Inputs may be any that keep to these rules, and one draw needn't show every extreme that they name: The span's tokens follow the first start cache positions of this sequence.
All inputs are finite; a program needn't handle non-finite values.
Results may differ from a plain program's by a relative error of at most 0.023.
Values may be sent and summed in bfloat16 or wider, within the bound.
A program may use at most 64 MiB of HBM per device.

v0:
```python
import math

import jax
import jax.numpy as jnp
import numpy as np
from jax import lax
from jax.sharding import PartitionSpec as P

D = 8192
QUERY_HEADS = 64
KEY_VALUE_HEADS = 8
HEAD_SIZE = 128


NEG_FILL = -1e30
EPSILON = 1e-05


def combined_all(value, axis, join):
    pieces = jax.tree.map(lambda part: lax.all_gather(part, axis), value)
    head = jax.tree.map(lambda part: part[0], pieces)
    tail = jax.tree.map(lambda part: part[1:], pieces)
    subtotal, _ = lax.scan(lambda subtotal, piece: (join(subtotal, piece), None), head, tail)
    return subtotal


def expand_heads(packed, key_value_table, head_dim):
    row_total = packed.shape[0]
    spread = packed.reshape(row_total, -1, head_dim)[:, key_value_table, :]
    return spread.reshape(row_total, key_value_table.shape[0] * head_dim)


def absorb(carried, scores, allowed, values):
    running_max, running_sum, weighted = carried
    masked = jnp.where(allowed, scores, NEG_FILL)
    new_peak = jnp.maximum(running_max, jnp.max(masked, axis=2))
    weights = jnp.where(allowed, jnp.exp(masked - new_peak[:, :, None]), 0.0)
    decay_factor = jnp.exp(running_max - new_peak)
    running_sum = running_sum * decay_factor + jnp.sum(weights, axis=2)
    update = jnp.einsum(
        "thk,kd->thd", weights.astype(jnp.bfloat16), values, preferred_element_type=jnp.float32
    )
    return (new_peak, running_sum, weighted * decay_factor[:, :, None] + update)


def join_parts(first_part, second_part):
    new_peak = jnp.maximum(first_part[0], second_part[0])
    first_scale = jnp.exp(first_part[0] - new_peak)
    second_scale = jnp.exp(second_part[0] - new_peak)
    joined_sum = first_part[1] * first_scale + second_part[1] * second_scale
    joined_values = (
        first_part[2] * first_scale[:, :, None] + second_part[2] * second_scale[:, :, None]
    )
    return (new_peak, joined_sum, joined_values)


def shards(
    queries,
    span_keys,
    span_head_values,
    prefix_cached_keys,
    prefix_cached_values,
    start,
    out_weight,
    residual,
    norm_gain,
    head_weight,
    targets,
):
    sequence_count = lax.axis_size("seq")
    voc_count = lax.axis_size("vocab")
    seq_rank = lax.axis_index("seq")
    voc_rank = lax.axis_index("vocab")
    present_heads = QUERY_HEADS // sequence_count
    key_value_table = np.arange(sequence_count) * present_heads // (QUERY_HEADS // KEY_VALUE_HEADS)
    wide_keys = expand_heads(span_keys, key_value_table, HEAD_SIZE)
    wide_values = expand_heads(span_head_values, key_value_table, HEAD_SIZE)
    head_queries, head_keys, head_values = (
        lax.all_to_all(queries, "seq", split_axis=1, concat_axis=0, tiled=True),
        lax.all_to_all(wide_keys, "seq", split_axis=1, concat_axis=0, tiled=True),
        lax.all_to_all(wide_values, "seq", split_axis=1, concat_axis=0, tiled=True),
    )
    held_keys, held_values = (
        lax.all_to_all(
            expand_heads(prefix_cached_keys, key_value_table, HEAD_SIZE),
            "seq",
            split_axis=1,
            concat_axis=0,
            tiled=True,
        ),
        lax.all_to_all(
            expand_heads(prefix_cached_values, key_value_table, HEAD_SIZE),
            "seq",
            split_axis=1,
            concat_axis=0,
            tiled=True,
        ),
    )
    token_count = head_queries.shape[0]
    query_block = head_queries.reshape(token_count, present_heads, HEAD_SIZE)
    score_scale = 1.0 / math.sqrt(HEAD_SIZE)
    cache_rows = prefix_cached_keys.shape[0]
    per_step = 1
    while (
        per_step * 2 <= sequence_count
        and sequence_count % (per_step * 2) == 0
        and (per_step * 2 * cache_rows <= 1024)
    ):
        per_step = per_step * 2
    steps_count = sequence_count // per_step
    step_keys = held_keys.reshape(steps_count, per_step * cache_rows, HEAD_SIZE)
    step_values = held_values.reshape(steps_count, per_step * cache_rows, HEAD_SIZE)
    within_step = jnp.arange(per_step * cache_rows, dtype=jnp.int32)
    live_count = start[0]

    def cache_step(carried, inputs):
        keys_here, values_here, step_id = inputs
        source = step_id * per_step + within_step // cache_rows
        positions = (source * voc_count + voc_rank) * cache_rows + within_step % cache_rows
        allowed = (positions < live_count)[None, None, :]
        scores = (
            jnp.einsum("thd,kd->thk", query_block, keys_here, preferred_element_type=jnp.float32)
            * score_scale
        )
        return (absorb(carried, scores, allowed, values_here), None)

    initial = (
        jnp.full((token_count, present_heads), NEG_FILL, jnp.float32),
        jnp.zeros((token_count, present_heads), jnp.float32),
        jnp.zeros((token_count, present_heads, HEAD_SIZE), jnp.float32),
    )
    carried, ignored = lax.scan(
        cache_step, initial, (step_keys, step_values, jnp.arange(steps_count, dtype=jnp.int32))
    )
    key_share = token_count // voc_count
    first_key = voc_rank * key_share
    own_keys = lax.dynamic_slice_in_dim(head_keys, first_key, key_share, 0)
    own_values = lax.dynamic_slice_in_dim(head_values, first_key, key_share, 0)
    key_ids = first_key + jnp.arange(key_share, dtype=jnp.int32)
    query_ids = jnp.arange(token_count, dtype=jnp.int32)
    allowed = (key_ids[None, :] <= query_ids[:, None])[:, None, :]
    scores = (
        jnp.einsum("thd,kd->thk", query_block, own_keys, preferred_element_type=jnp.float32)
        * score_scale
    )
    running_max, running_sum, weighted = absorb(carried, scores, allowed, own_values)
    running_max, running_sum, weighted = combined_all(
        (running_max, running_sum, weighted), "vocab", join_parts
    )
    attended = (
        (weighted / running_sum[:, :, None])
        .astype(jnp.bfloat16)
        .reshape(token_count, present_heads * HEAD_SIZE)
    )
    rows_in = attended
    projected = lax.psum_scatter(
        jnp.dot(rows_in, out_weight, preferred_element_type=jnp.float32).astype(jnp.bfloat16),
        "seq",
        scatter_dimension=0,
        tiled=True,
    ).astype(jnp.float32)
    hidden = (residual.astype(jnp.float32) + projected).astype(jnp.bfloat16)
    widened = hidden.astype(jnp.float32)
    squares = lax.psum(jnp.sum(widened * widened, axis=1), "vocab")
    normed = (widened * lax.rsqrt(squares / D + EPSILON)[:, None] * norm_gain[None, :]).astype(
        jnp.bfloat16
    )
    normed_all = lax.all_gather(normed, "seq", axis=0, tiled=True)
    rows_in = normed_all
    logits = lax.psum_scatter(
        jnp.dot(rows_in, head_weight, preferred_element_type=jnp.float32).astype(jnp.bfloat16),
        "vocab",
        scatter_dimension=0,
        tiled=True,
    ).astype(jnp.float32)
    vocab_here = head_weight.shape[1]
    offset = seq_rank * vocab_here
    is_target = jnp.arange(vocab_here, dtype=jnp.int32)[None, :] + offset == targets[:, None]
    target_part = jnp.sum(jnp.where(is_target, logits, 0.0), axis=1)
    local_peak = jnp.max(logits, axis=1)
    row_peak = lax.pmax(local_peak, "seq")
    local_total = jnp.sum(jnp.exp(logits - row_peak[:, None]), axis=1)
    row_total, picked = lax.psum((local_total, target_part), "seq")
    logprobs = picked - (row_peak + jnp.log(row_total))
    return (hidden, logprobs)


def solution(mesh):
    placed = (
        P("seq", None),
        P("seq", None),
        P("seq", None),
        P(("seq", "vocab"), None),
        P(("seq", "vocab"), None),
        P(),
        P("seq", "vocab"),
        P("seq", "vocab"),
        P("vocab"),
        P("vocab", "seq"),
        P("vocab"),
    )
    return jax.shard_map(
        shards,
        mesh=mesh,
        in_specs=placed,
        out_specs=(P("seq", "vocab"), P("vocab")),
        check_vma=False,
    )
```

profile of v0, /device:TPU:8, one launch (start us, length us, event | category | flops | bytes accessed | tf_op | source)
XLA Modules:
  0.0 837.3 jit_solution(4165556576637748645)
XLA Ops:
  9.9 11.7 %all-to-all-start.3 = ((bf16[16,32,128]{2,0,1:T(8,128)(2,1)}), bf16[16,32,128]{2,0,1:T(8,128)(2,1)S(1)}, u32[]{:S(2)}, u32[]{:S(2)}) async-start(bf16[16,32,128]{2,0,1:T(8,128)(2,1)} %bitcast.13), calls=%async_computation.3 | async-start | bytes 262144 | tf_op jit(solution)/shard_map/all_to_all | solution.py:80
  23.3 7.2 all-to-all-done.3
  31.1 5.3 all-to-all-start.1
  40.1 6.5 all-to-all-done.1
  46.7 5.8 all-to-all-start
  57.0 42.9 %all-to-all-done = bf16[256,32,128]{2,0,1:T(8,128)(2,1)S(1)} async-done(((bf16[256,32,128]{2,0,1:T(8,128)(2,1)}), bf16[256,32,128]{2,0,1:T(8,128)(2,1)S(1)}, u32[]{:S(2)}, u32[]{:S(2)}) %all-to-all-start) | async-done | bytes 2097184 | tf_op jit(solution)/shard_map/all_to_all | solution.py:84
  99.9 6.5 all-to-all-start.2
  108.8 44.5 %all-to-all-done.2 = bf16[256,32,128]{2,0,1:T(8,128)(2,1)} async-done(((bf16[256,32,128]{2,0,1:T(8,128)(2,1)}), bf16[256,32,128]{2,0,1:T(8,128)(2,1)}, u32[]{:S(2)}, u32[]{:S(2)}) %all-to-all-start.2) | async-done | bytes 2097184 | tf_op jit(solution)/shard_map/all_to_all | solution.py:91
  153.3 6.3 all-to-all-start.4
  159.6 92.4 %while.35 = (s32[]{:T(128)}, f32[512,2]{0,1:T(2,128)S(1)}, f32[512,2]{0,1:T(2,128)S(1)}, f32[512,2,128]{2,0,1:T(8,128)}, s32[8]{0:T(128)S(1)}, /*index=5*/s32[]{...) while((s32[]{:T(128)}, f32[512,2]{0,1:T(2,128)S(1)}, ...), condition=%wide.region_3.4_spmd.clone.clone, body=%wide.region_0.3_spmd.clone.clone.sunk | while | flops 550919168 | bytes 31268056 | solution.py:132
  179.1 3.5 fusion.98
  202.2 3.5 fusion.98
  237.0 3.5 fusion.98
  254.4 13.2 %all-gather = f32[4096,2]{0,1:T(2,128)S(1)} all-gather(f32[512,2]{0,1:T(2,128)S(1)} %max.16), channel_id=2, replica_groups=mesh['seq'=32,'vocab'=8] {'vocab'}, dimensions={0}, use_global_device_ids=true | all-gather | bytes 36864 | tf_op jit(solution)/shard_map/all_gather | solution.py:20
  267.6 13.0 %all-gather.1 = f32[4096,2]{0,1:T(2,128)S(1)} all-gather(f32[512,2]{0,1:T(2,128)S(1)} %get-tuple-element.456), channel_id=3, replica_groups=mesh['seq'=32,'vocab'=8] {'vocab'}, dimensions={0}, use_global_device_ids=true | all-gather | bytes 36864 | tf_op jit(solution)/shard_map/all_gather | solution.py:20
  280.6 9.6 %all-gather.8.cloned.1.call-done = f32[4096,2,128]{2,0,1:T(8,128)} async-done(((f32[512,2,128]{2,0,1:T(8,128)}), f32[4096,2,128]{2,0,1:T(8,128)}) %all-gather.8.cloned.1.call-update) | async-done | bytes 4194320 | tf_op jit(solution)/shard_map/all_gather | solution.py:20
  291.8 4.1 slice.43
  295.9 42.8 %while.34 = (s32[]{:T(128)}, f32[512,2]{0,1:T(2,128)S(1)}, f32[512,2]{0,1:T(2,128)S(1)}, f32[512,2,128]{2,1,0:T(2,128)S(1)}, f32[7,512,2]{1,2,0:T(2,128)S(1)}, /...) while((s32[]{:T(128)}, f32[512,2]{0,1:T(2,128)S(1)}, f32[512,2]{0,1:T(2,128)S(1)}, ...), condition=%wide.region_7.8_spmd, body=%wide.region_6.7_spmd.sunk | while | flops 399362 | bytes 2678885 | solution.py:23
  297.3 4.7 fusion.90
  303.4 4.7 fusion.90
  309.5 4.7 fusion.90
  315.6 4.7 fusion.90
  321.8 4.7 fusion.90
  327.9 4.7 fusion.90
  334.0 4.7 fusion.90
  341.1 213.9 %reduce-scatter.3.cloned.1.call-done = bf16[16,1024]{1,0:T(8,128)(2,1)} async-done(((bf16[512,1024]{1,0:T(8,128)(2,1)}), bf16[16,1024]{1,0:T(8,128)(2,1)}) %reduce-scatter.3.cloned.1.call-update) | async-done | bytes 32784 | tf_op jit(solution)/shard_map/reduce_scatter | solution.py:156
  555.9 12.4 %psum.21 = f32[16]{0:T(128)S(1)} all-reduce(f32[16]{0:T(128)S(1)} %get-tuple-element.454), channel_id=1, replica_groups=mesh['seq'=32,'vocab'=8] {'vocab'}, use_global_device_ids=true, to_apply=%region_10.11 | all-reduce | flops 16 | bytes 128 | tf_op jit(solution)/shard_map/psum | solution.py:164
  569.1 72.3 %all-gather.6.cloned.1.call-done = bf16[512,1024]{1,0:T(8,128)(2,1)} async-done(((bf16[16,1024]{1,0:T(8,128)(2,1)}), bf16[512,1024]{1,0:T(8,128)(2,1)}) %all-gather.6.cloned.1.call-update) | async-done | bytes 1048592 | tf_op jit(solution)/shard_map/all_gather | solution.py:168
  641.4 6.2 convolution_convert_fusion
  647.6 34.9 %reduce-scatter.5.cloned.1.call-done = bf16[64,2048]{1,0:T(8,128)(2,1)} async-done(((bf16[512,2048]{1,0:T(8,128)(2,1)}), bf16[64,2048]{1,0:T(8,128)(2,1)}) %reduce-scatter.5.cloned.1.call-update) | async-done | bytes 262160 | tf_op jit(solution)/shard_map/reduce_scatter | solution.py:170
  683.6 71.1 %pmax.7 = f32[64]{0:T(128)S(1)} all-reduce(bf16[64]{0:T(256)(128)(2,1)S(1)} %reduce_max.38), channel_id=1, replica_groups=mesh['seq'=32,'vocab'=8] {'seq'}, use_global_device_ids=true, to_apply=%region_15.16 | all-reduce | flops 64 | bytes 384 | tf_op jit(solution)/shard_map/pmax | solution.py:181
  756.0 74.2 %all-reduce = (f32[64]{0:T(128)S(1)}, f32[64]{0:T(128)S(1)}) all-reduce(f32[64]{0:T(128)S(1)} %get-tuple-element.411, f32[64]{0:T(128)S(1)} %get-tuple-element.410), channel_id=1, replica_groups=mesh['seq'=32,'vocab'=8] {'seq'}, use_global_device_ids=true, to_apply=%region_13.14 | all-reduce | flops 128 | bytes 1024 | tf_op jit(solution)/shard_map/psum | solution.py:183
  (183 shorter events, 112.8 us)
Async XLA Ops:
  7.2 332.4 %copy-start = (bf16[256,1024]{1,0:T(8,128)(2,1)S(1)}, bf16[256,1024]{1,0:T(8,128)(2,1)}, u32[]{:S(2)}) copy-start(bf16[256,1024]{1,0:T(8,128)(2,1)} %param.26) | copy-start | bytes 1572868
  9.9 20.6 %all-to-all-start.3 = ((bf16[16,32,128]{2,0,1:T(8,128)(2,1)}), bf16[16,32,128]{2,0,1:T(8,128)(2,1)S(1)}, u32[]{:S(2)}, u32[]{:S(2)}) async-start(bf16[16,32,128]{2,0,1:T(8,128)(2,1)} %bitcast.13), calls=%async_computation.3 | async-start | bytes 262144 | tf_op jit(solution)/shard_map/all_to_all | solution.py:80
  30.5 0.7 copy-start.5
  31.1 15.6 %all-to-all-start.1 = ((bf16[16,32,256]{2,0,1:T(8,128)(2,1)}), bf16[16,32,256]{2,0,1:T(8,128)(2,1)S(1)}, u32[]{:S(2)}, u32[]{:S(2)}) async-start(bf16[16,32,256]{2,0,1:T(8,128)(2,1)} %bitcast.99), calls=%async_computation.1 | async-start | bytes 524288 | tf_op jit(solution)/shard_map/all_to_all | solution.py:79
  38.0 14.5 %copy-start.4 = (bf16[256,1024]{1,0:T(8,128)(2,1)S(1)}, bf16[256,1024]{1,0:T(8,128)(2,1)}, u32[]{:S(2)}) copy-start(bf16[256,1024]{1,0:T(8,128)(2,1)} %param.24) | copy-start | bytes 1572868
  46.7 10.3 %copy-start.2 = (bf16[16,32,256]{2,0,1:T(8,128)(2,1)}, bf16[16,32,256]{2,0,1:T(8,128)(2,1)S(1)}, u32[]{:S(2)}) copy-start(bf16[16,32,256]{2,0,1:T(8,128)(2,1)S(1)} %all-to-all-done.1) | copy-start | bytes 786436
  46.7 53.2 %all-to-all-start = ((bf16[256,32,128]{2,0,1:T(8,128)(2,1)}), bf16[256,32,128]{2,0,1:T(8,128)(2,1)S(1)}, u32[]{:S(2)}, u32[]{:S(2)}) async-start(bf16[256,32,128]{2,0,1:T(8,128)(2,1)} %bitcast.5), calls=%async_computation | async-start | bytes 4194304 | tf_op jit(solution)/shard_map/all_to_all | solution.py:84
  54.8 51.6 %copy-start.8 = (bf16[16,1024]{1,0:T(8,128)(2,1)S(1)}, bf16[16,1024]{1,0:T(8,128)(2,1)}, u32[]{:S(2)}) copy-start(bf16[16,1024]{1,0:T(8,128)(2,1)} %param.22) | copy-start | bytes 98308
  99.9 7.9 copy-start.3
  99.9 53.4 %all-to-all-start.2 = ((bf16[256,32,128]{2,0,1:T(8,128)(2,1)}), bf16[256,32,128]{2,0,1:T(8,128)(2,1)}, u32[]{:S(2)}, u32[]{:S(2)}) async-start(bf16[256,32,128]{2,0,1:T(8,128)(2,1)} %bitcast.10), calls=%async_computation.2 | async-start | bytes 4194304 | tf_op jit(solution)/shard_map/all_to_all | solution.py:91
  153.3 98.9 %all-to-all-start.4 = ((bf16[16,32,128]{2,0,1:T(8,128)(2,1)}), bf16[16,32,128]{2,0,1:T(8,128)(2,1)S(1)}, u32[]{:S(2)}, u32[]{:S(2)}) async-start(bf16[16,32,128]{2,0,1:T(8,128)(2,1)} %bitcast.18), calls=%async_computation.4 | async-start | bytes 262144 | tf_op jit(solution)/shard_map/all_to_all | solution.py:81
  159.6 130.7 %all-gather.8.cloned.1.call-start = ((), (), s32[]{:S(2)}) async-start(), calls=%async_computation.10 | async-start | bytes 4718592 | tf_op jit(solution)/shard_map/all_gather | solution.py:20
  164.2 3.5 copy-start.1
  175.6 3.5 copy-start.1
  187.2 3.5 copy-start.1
  198.8 3.5 copy-start.1
  210.4 3.5 copy-start.1
  221.9 3.5 copy-start.1
  233.5 3.5 copy-start.1
  245.1 3.5 copy-start.1
  254.4 300.6 %reduce-scatter.3.cloned.1.call-start = ((), (), s32[]{:S(2)}) async-start(), calls=%async_computation.7 | async-start | bytes 1081344 | tf_op jit(solution)/shard_map/reduce_scatter | solution.py:156
  338.7 216.3 %copy-start.7 = (bf16[16,1024]{1,0:T(8,128)(2,1)S(1)}, bf16[16,1024]{1,0:T(8,128)(2,1)}, u32[]{:S(2)}) copy-start(bf16[16,1024]{1,0:T(8,128)(2,1)} %param.27) | copy-start | bytes 98308
  338.7 229.6 %copy-start.9 = (f32[1024]{0:T(1024)S(1)}, f32[1024]{0:T(1024)}, u32[]{:S(2)}) copy-start(f32[1024]{0:T(1024)} %param.28) | copy-start | bytes 12292
  341.0 300.3 %all-gather.6.cloned.1.call-start = ((), (), s32[]{:S(2)}) async-start(), calls=%async_computation.8 | async-start | bytes 1081344 | tf_op jit(solution)/shard_map/all_gather | solution.py:168
  555.9 91.7 %copy-start.6 = (bf16[16,1024]{1,0:T(8,128)(2,1)}, bf16[16,1024]{1,0:T(8,128)(2,1)S(1)}, u32[]{:S(2)}) copy-start(bf16[16,1024]{1,0:T(8,128)(2,1)S(1)} %get-tuple-element.455) | copy-start | bytes 98308
  569.0 185.7 %copy-start.10 = (s32[64]{0:T(128)S(1)}, s32[64]{0:T(128)}, u32[]{:S(2)}) copy-start(s32[64]{0:T(128)} %param.30) | copy-start | bytes 772
  569.0 113.4 %reduce-scatter.5.cloned.1.call-start = ((), (), s32[]{:S(2)}) async-start(), calls=%async_computation.9 | async-start | bytes 2359296 | tf_op jit(solution)/shard_map/reduce_scatter | solution.py:170
Sparse Core Ops, SparseCore 0:
  254.5 35.7 all-gather.7
  341.1 213.7 reduce-scatter.2
  569.1 72.1 all-gather.5
  647.7 34.7 reduce-scatter.4
where the time goes:
time: 839 us; the launch traced here: 837 us
  waiting for transfers between devices  432 us (51%)
  blocking collectives  184 us (22%)
  other arithmetic  69.1 us (8%)
  matrix products  60.1 us (7%)
  local copies, waits for them, and re-layouts  36.9 us (4%)
  starting transfers between devices  35.7 us (4%)
  between operations  14.1 us (2%)
    reduce_scatter x1, waiting for transfers between devices, shards(): lax.psum_scatter(jnp.dot(rows_in, out_weight, preferred_element_type=jnp....  214 us
    psum x1, blocking collectives, shards(): row_total, picked = lax.psum((local_total, target_part), 'seq')  74.2 us
    all_gather x1, waiting for transfers between devices, shards(): normed_all = lax.all_gather(normed, 'seq', axis=0, tiled=True)  72.3 us
    pmax x1, blocking collectives, shards(): row_peak = lax.pmax(local_peak, 'seq')  71.1 us
    all_to_all x1, waiting for transfers between devices, shards(): lax.all_to_all(expand_heads(prefix_cached_values, key_value_table, HEAD_S...  44.5 us
    all_to_all x1, waiting for transfers between devices, shards(): lax.all_to_all(expand_heads(prefix_cached_keys, key_value_table, HEAD_SIZ...  42.9 us
    reduce_scatter x1, waiting for transfers between devices, shards(): lax.psum_scatter(jnp.dot(rows_in, head_weight, preferred_element_type=jnp...  34.9 us
    add x7, other arithmetic, join_parts(): first_part[2] * first_scale[:, :, None]  32.6 us
  transfers between devices with their start and end apart: 9, of which 8 were waited for; matrix products, arithmetic and copies ran while one was open for 12% of the time, Pallas kernels for 0%

commit v1 on v0

v1 whole, which is shorter than its diff:
```python
import functools
import math

import jax
import jax.numpy as jnp
from jax import lax
from jax.experimental import pallas as pl
from jax.experimental.pallas import tpu as pltpu
from jax.sharding import PartitionSpec as P

D = 8192
HEADS = 8
HS = 128
NY, NZ, NX = 4, 8, 4
NV = 2 * NX
ROWS = 16
CACHE = 256
KEYS = NV * CACHE
KEYS_PAD = KEYS + 128
GW = HEADS * HS
PW = GW + 128
VOC = 2048
TILE = 512
NT = VOC // TILE
FEAT = 256
BIG_NEG = -1e30
EPSILON = 1e-05
MESH = pl.DeviceIdType.MESH
BF = jnp.bfloat16
F32 = jnp.float32


class Place:
    def __init__(self):
        s, v = lax.axis_index("seq"), lax.axis_index("vocab")
        self.s, self.v = s, v
        self.z, self.y = lax.div(s, NY), lax.rem(s, NY)
        self.x, self.c = lax.div(v, 2), lax.rem(v, 2)

    def yy(self, d):
        return lax.rem(self.y + d + NY, NY)

    def zz(self, d):
        return lax.rem(self.z + d + NZ, NZ)

    def xx(self, d):
        return lax.rem(self.x + d + NX, NX)

    def at_z(self, d):
        return (self.zz(d) * NY + self.y, self.v)

    def at_y(self, d):
        return (self.z * NY + self.yy(d), self.v)

    def at_x(self, d, core):
        return (self.s, self.xx(d) * 2 + core)

    def at_v(self, d):
        return (self.s, lax.rem(self.v + d, NV))


def rdma(src, dst, send, recv, dev):
    return pltpu.make_async_remote_copy(
        src_ref=src, dst_ref=dst, send_sem=send, recv_sem=recv, device_id=dev, device_id_type=MESH
    )


def greet(partners, extra=()):
    bar = pltpu.get_barrier_semaphore()
    for dev in partners:
        pl.semaphore_signal(bar, inc=1, device_id=dev, device_id_type=MESH)
    count = len(partners)
    for use, dev in extra:

        @pl.when(use)
        def _():
            pl.semaphore_signal(bar, inc=1, device_id=dev, device_id_type=MESH)

        count = count + use.astype(jnp.int32)
    pl.semaphore_wait(bar, count)


def seq_partners(me):
    return [me.at_z(d) for d in range(1, NZ)] + [me.at_y(1), me.at_y(-1)]


def gather_seq(me, buf, zs, zr, ys, yr, fs, fr):
    half = buf.shape[3] // 2
    sends = []

    def go(cp):
        cp.start()
        sends.append(cp)

    own = buf.at[me.y, me.z]
    for d in range(1, NZ):
        go(rdma(own, own, zs.at[d - 1], zr.at[d - 1], me.at_z(d)))
    for step in range(NZ + 1):
        if step < NZ:
            zz = me.zz(-step)
            blk = buf.at[me.y, zz]
            if step:
                rdma(blk, blk, zs.at[step - 1], zr.at[step - 1], me.at_z(1)).wait_recv()
            go(rdma(blk, blk, ys.at[0, step], yr.at[0, step], me.at_y(1)))
            go(rdma(blk, blk, ys.at[1, step], yr.at[1, step], me.at_y(-1)))
        if step:
            d = step - 1
            zz = me.zz(-d)
            for k, way in ((0, 1), (1, -1)):
                blk = buf.at[me.yy(-way), zz]
                rdma(blk, blk, ys.at[k, d], yr.at[k, d], me.at_y(way)).wait_recv()
                part = buf.at[me.yy(-way), zz, :, pl.ds(k * half, half)]
                go(rdma(part, part, fs.at[k, d], fr.at[k, d], me.at_y(way)))
    for d in range(NZ):
        zz = me.zz(-d)
        for k in range(2):
            part = buf.at[me.yy(2), zz, :, pl.ds(k * half, half)]
            rdma(part, part, fs.at[k, d], fr.at[k, d], me.at_y(1)).wait_recv()
    return sends


GATHER_SEMS = [
    pltpu.SemaphoreType.DMA((NZ - 1,)),
    pltpu.SemaphoreType.DMA((NZ - 1,)),
    pltpu.SemaphoreType.DMA((2, NZ)),
    pltpu.SemaphoreType.DMA((2, NZ)),
    pltpu.SemaphoreType.DMA((2, NZ)),
    pltpu.SemaphoreType.DMA((2, NZ)),
]


def reduce_seq(me, part, r1, r2, mg, rz, ss, rs, zs, zr, join, last):
    width = part.shape[3]
    hz = NZ // 2
    sends = []

    def go(cp):
        cp.start()
        sends.append(cp)

    far = me.yy(2)
    for k, way in ((0, 1), (1, -1)):
        half = pl.ds(k * hz, hz)
        go(rdma(part.at[far, half], r1.at[k], ss.at[k, 0], rs.at[k, 0], me.at_y(way)))
    for k, way in ((0, 1), (1, -1)):
        other = pl.ds((1 - k) * hz, hz)
        go(rdma(part.at[me.yy(way), other], r2.at[k, other], ss.at[k, 1], rs.at[k, 1], me.at_y(way)))
    for k, way in ((0, 1), (1, -1)):
        rdma(r1.at[k], r1.at[k], ss.at[k, 0], rs.at[k, 0], me.at_y(way)).wait_recv()
        half = pl.ds(k * hz, hz)
        mine = part[me.yy(way), half].reshape(hz * ROWS, width)
        got = r1[k].reshape(hz * ROWS, width)
        part[me.yy(way), half] = join([mine, got]).reshape(hz, ROWS, width)
        go(rdma(part.at[me.yy(way), half], r2.at[k, half], ss.at[k, 2], rs.at[k, 2], me.at_y(way)))
    for k, way in ((0, 1), (1, -1)):
        for i in range(2):
            half = pl.ds((k if i else 1 - k) * hz, hz)
            blk = r2.at[k, half]
            rdma(blk, blk, ss.at[k, 1 + i], rs.at[k, 1 + i], me.at_y(way)).wait_recv()
    items = [part[me.y].reshape(NZ * ROWS, width)]
    items += [r2[k].reshape(NZ * ROWS, width) for k in range(2)]
    mg[...] = join(items).reshape(NZ, ROWS, width)
    for d in range(1, NZ):
        go(rdma(mg.at[me.zz(d)], rz.at[d - 1], zs.at[d - 1], zr.at[d - 1], me.at_z(d)))
    items = [mg[me.z]]
    for d in range(1, NZ):
        blk = rz.at[d - 1]
        rdma(blk, blk, zs.at[d - 1], zr.at[d - 1], me.at_z(d)).wait_recv()
        items.append(rz[d - 1])
    return last(items), sends


def reduce_scratch(width):
    return [
        pltpu.VMEM((2, NZ // 2, ROWS, width), BF),
        pltpu.VMEM((2, NZ, ROWS, width), BF),
        pltpu.VMEM((NZ, ROWS, width), BF),
        pltpu.VMEM((NZ - 1, ROWS, width), BF),
        pltpu.SemaphoreType.DMA((2, 3)),
        pltpu.SemaphoreType.DMA((2, 3)),
        pltpu.SemaphoreType.DMA((NZ - 1,)),
        pltpu.SemaphoreType.DMA((NZ - 1,)),
    ]


def lanes(shape):
    return lax.broadcasted_iota(jnp.int32, shape, len(shape) - 1)


def pack_lse(lse, low8):
    second = pltpu.roll(lse, 8, 1) if low8 else lse
    third = pltpu.roll(lse, 16, 1) if low8 else lse

    def split(a):
        hi = a.astype(BF).astype(F32)
        mid = (a - hi).astype(BF).astype(F32)
        return hi, mid, a - hi - mid

    lane = lanes(lse.shape)
    out = jnp.where(lane < 8, split(lse)[0], jnp.where(lane < 16, split(second)[1], split(third)[2]))
    return jnp.where(lane < 24, out, 0.0).astype(BF)


def unpack_lse(packed):
    a = packed.astype(F32)
    return a + (pltpu.roll(a, 120, 1) + pltpu.roll(a, 112, 1))


def join_partials(items, final=False):
    lses = [unpack_lse(it[:, GW:]) for it in items]
    peak = functools.reduce(jnp.maximum, lses)
    weights = [jnp.exp2(l - peak) for l in lses]
    total = functools.reduce(jnp.add, weights)
    weights = [w / total for w in weights]
    cols = []
    for h in range(HEADS):
        acc = None
        for w, it in zip(weights, items):
            term = w[:, h : h + 1] * it[:, h * HS : (h + 1) * HS].astype(F32)
            acc = term if acc is None else acc + term
        cols.append(acc.astype(BF))
    if not final:
        cols.append(pack_lse(peak + jnp.log2(total), True))
    return jnp.concatenate(cols, axis=1)


def attention_kernel(
    q_ref, sk_ref, sv_ref, ck_ref, cv_ref, start_ref, out_ref,
    qall, kbuf, vbuf, vext, krel, vrel, bias, lse_buf, opart,
    gz, gzr, gy, gyr, gf, gfr, loc, kvs, kr, vr, rels, relr, fws,
    r1, r2, mg, rz, rss, rsr, rzs, rzr,
):
    me = Place()
    sends = []

    def go(cp):
        cp.start()
        sends.append(cp)

    head_cols = pl.ds(pl.multiple_of(me.v * GW, GW), GW)
    own_q = pltpu.make_async_copy(q_ref.at[:, head_cols], qall.at[me.y, me.z], loc.at[0])
    own_q.start()

    def cols(vv):
        return pl.ds(pl.multiple_of(vv * HS, HS), HS)

    def rows(vv):
        return pl.ds(pl.multiple_of(vv * CACHE, CACHE), CACHE)

    own_k = pltpu.make_async_copy(ck_ref.at[:, cols(me.v)], kbuf.at[rows(me.v)], kr.at[me.v])
    own_v = pltpu.make_async_copy(cv_ref.at[:, cols(me.v)], vbuf.at[rows(me.v)], vr.at[me.v])
    own_k.start()
    own_v.start()
    kbuf[KEYS:, :] = jnp.zeros((128, HS), BF)
    vbuf[KEYS:, :] = jnp.zeros((128, HS), BF)
    kbuf[KEYS : KEYS + ROWS, :] = sk_ref[:, cols(me.v)]
    vbuf[KEYS : KEYS + ROWS, :] = sv_ref[:, cols(me.v)]
    own_q.wait()
    near = [(0, 1 - me.c), (1, 0), (1, 1), (-1, 0), (-1, 1)]
    greet(seq_partners(me) + [me.at_x(d, c) for d, c in near])

    farx = me.xx(2)
    far_cols = pl.ds(pl.multiple_of(farx * 2 * HS, 2 * HS), 2 * HS)
    go(rdma(ck_ref.at[:, far_cols], krel, rels.at[0], relr.at[0], me.at_x(1, me.c)))
    go(rdma(cv_ref.at[:, far_cols], vrel, rels.at[1], relr.at[1], me.at_x(-1, me.c)))
    for i, (d, c) in enumerate(near):
        vv = me.xx(d) * 2 + c
        go(rdma(ck_ref.at[:, cols(vv)], kbuf.at[rows(me.v)], kvs.at[0, i], kr.at[me.v], me.at_x(d, c)))
        go(rdma(cv_ref.at[:, cols(vv)], vbuf.at[rows(me.v)], kvs.at[1, i], vr.at[me.v], me.at_x(d, c)))

    sends += gather_seq(me, qall, gz, gzr, gy, gyr, gf, gfr)

    rdma(krel, krel, rels.at[0], relr.at[0], me.at_x(1, me.c)).wait_recv()
    src = me.xx(-1) * 2 + me.c
    for c in range(2):
        go(rdma(krel.at[:, pl.ds(c * HS, HS)], kbuf.at[rows(src)], fws.at[0, c], kr.at[src], me.at_x(1, c)))
    rdma(vrel, vrel, rels.at[1], relr.at[1], me.at_x(-1, me.c)).wait_recv()
    src = me.xx(1) * 2 + me.c
    for c in range(2):
        go(rdma(vrel.at[:, pl.ds(c * HS, HS)], vbuf.at[rows(src)], fws.at[1, c], vr.at[src], me.at_x(-1, c)))

    flat = lanes((1, KEYS_PAD))
    bias[...] = jnp.where(flat < start_ref[0] - me.s * KEYS, 0.0, BIG_NEG)
    own_k.wait()
    own_v.wait()
    for d in range(1, NV):
        src = lax.rem(me.v + d, NV)
        blk = kbuf.at[rows(src)]
        rdma(blk, blk, kvs.at[0, 0], kr.at[src], me.at_v(1)).wait_recv()
        blk = vbuf.at[rows(src)]
        rdma(blk, blk, kvs.at[1, 0], vr.at[src], me.at_v(1)).wait_recv()
    vext[:, :HS] = vbuf[...]
    vext[:, HS:] = jnp.ones((KEYS_PAD, HS), BF)

    scale = math.log2(math.e) / math.sqrt(HS)
    nrow = NZ * ROWS
    for order in (2, 1, 3, 0):
        yy = me.yy(order)

        def pair(hp, carry):
            both = []
            for i in range(2):
                at = pl.ds(pl.multiple_of((hp * 2 + i) * HS, HS), HS)
                both.append(qall[yy, :, :, at].reshape(nrow, HS))
            q2 = jnp.concatenate(both, axis=0)
            sc = lax.dot_general(q2, kbuf[...], (((1,), (1,)), ((), ())), preferred_element_type=F32)
            main = sc[:, :KEYS] * scale + bias[:, :KEYS]
            row = lax.broadcasted_iota(jnp.int32, (2 * nrow, 128), 0)
            row = lax.rem(row, nrow)
            token = lax.div(row, ROWS) * (NY * ROWS) + yy * ROWS + lax.rem(row, ROWS)
            key = lanes((2 * nrow, 128))
            ok = (key < ROWS) & (key + me.s * ROWS <= token)
            span = jnp.where(ok, sc[:, KEYS:] * scale, BIG_NEG)
            peak = jnp.maximum(
                jnp.max(main, axis=1, keepdims=True), jnp.max(span, axis=1, keepdims=True)
            )
            pm = jnp.exp2(main - peak).astype(BF)
            ps = jnp.exp2(span - peak).astype(BF)
            ps = jnp.where(ok, ps, jnp.zeros_like(ps))
            o = jnp.dot(pm, vext[:KEYS, :], preferred_element_type=F32)
            o = o + jnp.dot(ps, vext[KEYS:, :], preferred_element_type=F32)
            total = o[:, HS:]
            total = jnp.where(total > 0.0, total, 1.0)
            on = (o[:, :HS] / total).astype(BF)
            lse = peak + jnp.log2(total)
            lane = lanes((nrow, 128))
            for i in range(2):
                h = hp * 2 + i
                at = pl.ds(pl.multiple_of(h * HS, HS), HS)
                opart[yy, :, :, at] = on[i * nrow : (i + 1) * nrow].reshape(NZ, ROWS, HS)
                mine = lse[i * nrow : (i + 1) * nrow]
                lse_buf[...] = jnp.where(lax.rem(lane, 8) == h, mine, lse_buf[...])
            return carry

        lax.fori_loop(0, HEADS // 2, pair, 0)
        opart[yy, :, :, GW:] = pack_lse(lse_buf[...], False).reshape(NZ, ROWS, 128)

    joined, more = reduce_seq(
        me, opart, r1, r2, mg, rz, rss, rsr, rzs, rzr,
        join_partials, functools.partial(join_partials, final=True),
    )
    out_ref[...] = joined
    for cp in sends + more:
        cp.wait_send()


def add_partials(items):
    return functools.reduce(jnp.add, [it.astype(F32) for it in items]).astype(BF)


def add_last(items):
    return functools.reduce(jnp.add, [it.astype(F32) for it in items])


def project_kernel(
    att_ref, w_ref, res_ref, gain_ref, hid_ref, nall_ref,
    tin, aall, opart, sq, nall, tss, trs, avs, avr, sqs, sqr,
    gz, gzr, gy, gyr, gf, gfr,
    r1, r2, mg, rz, rss, rsr, rzs, rzr,
):
    me = Place()
    sends = []

    def go(cp):
        cp.start()
        sends.append(cp)

    same = [(me.z == me.v) & (me.y == j) for j in range(NY)]
    across = [(me.v * NY + j, me.z) for j in range(NY)]
    greet(
        seq_partners(me) + [me.at_v(d) for d in range(1, NV)],
        [(jnp.logical_not(same[j]), across[j]) for j in range(NY)],
    )

    turns = []
    for j in range(NY):
        src = att_ref.at[:, pl.ds(j * FEAT, FEAT)]
        cp = rdma(src, tin.at[me.y], tss.at[j], trs.at[me.y], across[j])
        loc = pltpu.make_async_copy(src, tin.at[me.y], trs.at[me.y])

        @pl.when(jnp.logical_not(same[j]))
        def _():
            cp.start()

        @pl.when(same[j])
        def _():
            loc.start()

        turns.append((jnp.logical_not(same[j]), cp))
    for j in range(NY):
        blk = tin.at[j]
        rdma(blk, blk, tss.at[j], trs.at[j], across[0]).wait_recv()
    aall[me.v] = tin[...]
    for d in range(1, NV):
        go(rdma(tin, aall.at[me.v], avs.at[d - 1], avr.at[d - 1], me.at_v(d)))
    for d in range(1, NV):
        blk = aall.at[lax.rem(me.v - d + NV, NV)]
        rdma(blk, blk, avs.at[d - 1], avr.at[d - 1], me.at_v(1)).wait_recv()

    nrow = NZ * ROWS
    for order in (2, 1, 3, 0):
        yy = me.yy(order)
        a = aall[:, yy].reshape(nrow, FEAT)
        opart[yy] = jnp.dot(a, w_ref[...], preferred_element_type=F32).astype(BF).reshape(NZ, ROWS, GW)
    projected, more = reduce_seq(
        me, opart, r1, r2, mg, rz, rss, rsr, rzs, rzr, add_partials, add_last
    )
    sends += more
    hidden = (res_ref[...].astype(F32) + projected).astype(BF)
    hid_ref[...] = hidden
    wide = hidden.astype(F32)
    sq[me.v] = jnp.broadcast_to(jnp.sum(wide * wide, axis=1, keepdims=True), (ROWS, 128))
    for d in range(1, NV):
        go(rdma(sq.at[me.v], sq.at[me.v], sqs.at[d - 1], sqr.at[d - 1], me.at_v(d)))
    for d in range(1, NV):
        blk = sq.at[lax.rem(me.v - d + NV, NV)]
        rdma(blk, blk, sqs.at[d - 1], sqr.at[d - 1], me.at_v(1)).wait_recv()
    mean = jnp.sum(sq[...], axis=0)[:, :1] * (1.0 / D)
    nall[me.y, me.z] = (wide * lax.rsqrt(mean + EPSILON) * gain_ref[...]).astype(BF)
    sends += gather_seq(me, nall, gz, gzr, gy, gyr, gf, gfr)
    nall_ref[...] = nall[...]
    for use, cp in turns:

        @pl.when(use)
        def _():
            cp.wait_send()

    for cp in sends:
        cp.wait_send()


def logits_kernel(
    n_ref, hw_ref, tgt_ref, out_ref,
    osend, orecv, own, sx, x1, x2, sty, stz, cs, cr, xs, xr, yss, yrs, zss, zrs,
):
    me = Place()
    sends = []

    def go(cp):
        cp.start()
        sends.append(cp)

    greet(
        [me.at_z(d) for d in range(1, NZ)]
        + [me.at_y(d) for d in range(1, NY)]
        + [me.at_x(0, 1 - me.c), me.at_x(1, me.c), me.at_x(-1, me.c)]
    )
    tok = NY * ROWS
    shift = (2, 1, 3, 0)

    def rows_of(core):
        blocks = []
        for d in shift:
            for y in range(NY):
                blocks.append(n_ref[y, me.xx(d) * 2 + core])
        return jnp.concatenate(blocks, axis=0)

    sib = me.at_x(0, 1 - me.c)
    lhs = rows_of(1 - me.c)
    for n in range(NT):
        at = pl.ds(n * TILE, TILE)
        osend[n] = (
            jnp.dot(lhs, hw_ref[:, at], preferred_element_type=F32).astype(BF).reshape(NX, tok, TILE)
        )
        go(rdma(osend.at[n], orecv.at[n], cs.at[n], cr.at[n], sib))
    lhs = rows_of(me.c)
    hr = tok // 2
    for n in range(NT):
        at = pl.ds(n * TILE, TILE)
        mine = jnp.dot(lhs, hw_ref[:, at], preferred_element_type=F32).reshape(NX, tok, TILE)
        rdma(orecv.at[n], orecv.at[n], cs.at[n], cr.at[n], sib).wait_recv()
        own[n] = mine + orecv[n].astype(F32)
        sx[n] = own[n, :3].astype(BF)
        for k, way in ((0, 1), (1, -1)):
            half = pl.ds(k * hr, hr)
            go(rdma(sx.at[n, 0, half], x1.at[k, n], xs.at[k, 0, n], xr.at[k, 0, n], me.at_x(way, me.c)))
        for k, way in ((0, 1), (1, -1)):
            half = pl.ds((1 - k) * hr, hr)
            go(rdma(sx.at[n, 1 + k, half], x2.at[k, n, half], xs.at[k, 1, n], xr.at[k, 1, n], me.at_x(way, me.c)))
    for n in range(NT):
        for k, way in ((0, 1), (1, -1)):
            blk = x1.at[k, n]
            rdma(blk, blk, xs.at[k, 0, n], xr.at[k, 0, n], me.at_x(way, me.c)).wait_recv()
            half = pl.ds(k * hr, hr)
            sx[n, 1 + k, half] = (own[n, 1 + k, half] + x1[k, n].astype(F32)).astype(BF)
            go(rdma(sx.at[n, 1 + k, half], x2.at[k, n, half], xs.at[k, 2, n], xr.at[k, 2, n], me.at_x(way, me.c)))

    tgt = jnp.broadcast_to(tgt_ref[...].astype(F32), (128, 128))
    tgt = jnp.transpose(tgt)[:tok, :1].astype(jnp.int32) - me.s * VOC
    tiles, peak = [], None
    for n in range(NT):
        for k, way in ((0, 1), (1, -1)):
            for i in range(2):
                half = pl.ds((k if i else 1 - k) * hr, hr)
                blk = x2.at[k, n, half]
                rdma(blk, blk, xs.at[k, 1 + i, n], xr.at[k, 1 + i, n], me.at_x(way, me.c)).wait_recv()
        lg = own[n, 3] + x2[0, n].astype(F32) + x2[1, n].astype(F32)
        own[n, 3] = lg
        top = jnp.max(lg, axis=1, keepdims=True)
        peak = top if peak is None else jnp.maximum(peak, top)
    total = picked = None
    for n in range(NT):
        lg = own[n, 3]
        a = jnp.sum(jnp.exp(lg - peak), axis=1, keepdims=True)
        b = jnp.sum(jnp.where(lanes((tok, TILE)) + n * TILE == tgt, lg, 0.0), axis=1, keepdims=True)
        total = a if total is None else total + a
        picked = b if picked is None else picked + b
    lane = lanes((tok, 128))
    st = jnp.where(lane == 0, peak, jnp.where(lane == 1, total, picked))
    st = jnp.concatenate([st, jnp.zeros((128 - tok, 128), F32)], axis=0)
    sty[0] = jnp.transpose(st)[:8]

    def joined(buf, count):
        top = functools.reduce(jnp.maximum, [buf[i, 0:1] for i in range(count)])
        tot = functools.reduce(jnp.add, [buf[i, 1:2] * jnp.exp(buf[i, 0:1] - top) for i in range(count)])
        pick = functools.reduce(jnp.add, [buf[i, 2:3] for i in range(count)])
        return top, tot, pick

    for d in range(1, NY):
        go(rdma(sty.at[0], sty.at[d], yss.at[d - 1], yrs.at[d - 1], me.at_y(d)))
    for d in range(1, NY):
        rdma(sty.at[d], sty.at[d], yss.at[d - 1], yrs.at[d - 1], me.at_y(d)).wait_recv()
    top, tot, pick = joined(sty, NY)
    stz[0] = jnp.concatenate([top, tot, pick, jnp.zeros((5, 128), F32)], axis=0)
    for d in range(1, NZ):
        go(rdma(stz.at[0], stz.at[d], zss.at[d - 1], zrs.at[d - 1], me.at_z(d)))
    for d in range(1, NZ):
        rdma(stz.at[d], stz.at[d], zss.at[d - 1], zrs.at[d - 1], me.at_z(d)).wait_recv()
    top, tot, pick = joined(stz, NZ)
    out_ref[...] = (pick - (top + jnp.log(tot)))[:, :tok]
    for cp in sends:
        cp.wait_send()


def vm():
    return pl.BlockSpec(memory_space=pltpu.VMEM)


def params(cid):
    return pltpu.CompilerParams(
        collective_id=cid, has_side_effects=True, vmem_limit_bytes=56 * 1024 * 1024
    )


def dma(*shape):
    return pltpu.SemaphoreType.DMA(shape)


def shards(q, sk, sv, ck, cv, start, w, res, gain, hw, tgt):
    any_ = pl.BlockSpec(memory_space=pl.ANY)
    att = pl.pallas_call(
        attention_kernel,
        out_shape=jax.ShapeDtypeStruct((ROWS, GW), BF),
        in_specs=[any_, vm(), vm(), any_, any_, pl.BlockSpec(memory_space=pltpu.SMEM)],
        out_specs=vm(),
        scratch_shapes=[
            pltpu.VMEM((NY, NZ, ROWS, GW), BF),
            pltpu.VMEM((KEYS_PAD, HS), BF),
            pltpu.VMEM((KEYS_PAD, HS), BF),
            pltpu.VMEM((KEYS_PAD, 2 * HS), BF),
            pltpu.VMEM((CACHE, 2 * HS), BF),
            pltpu.VMEM((CACHE, 2 * HS), BF),
            pltpu.VMEM((1, KEYS_PAD), F32),
            pltpu.VMEM((NZ * ROWS, 128), F32),
            pltpu.VMEM((NY, NZ, ROWS, PW), BF),
        ]
        + GATHER_SEMS
        + [dma(1), dma(2, 5), dma(NV), dma(NV), dma(2), dma(2), dma(2, 2)]
        + reduce_scratch(PW),
        compiler_params=params(0),
        name="attention",
    )(q, sk, sv, ck, cv, start)
    hidden, normed = pl.pallas_call(
        project_kernel,
        out_shape=(
            jax.ShapeDtypeStruct((ROWS, GW), BF),
            jax.ShapeDtypeStruct((NY, NZ, ROWS, GW), BF),
        ),
        in_specs=[vm()] * 4,
        out_specs=(vm(), vm()),
        scratch_shapes=[
            pltpu.VMEM((NY, ROWS, FEAT), BF),
            pltpu.VMEM((NV, NY, ROWS, FEAT), BF),
            pltpu.VMEM((NY, NZ, ROWS, GW), BF),
            pltpu.VMEM((NV, ROWS, 128), F32),
            pltpu.VMEM((NY, NZ, ROWS, GW), BF),
            dma(NY), dma(NY), dma(NV - 1), dma(NV - 1), dma(NV - 1), dma(NV - 1),
        ]
        + GATHER_SEMS
        + reduce_scratch(GW),
        compiler_params=params(1),
        name="project",
    )(att, w, res, gain.reshape(1, GW))
    tok = NY * ROWS
    logprobs = pl.pallas_call(
        logits_kernel,
        out_shape=jax.ShapeDtypeStruct((1, tok), F32),
        in_specs=[vm()] * 3,
        out_specs=vm(),
        scratch_shapes=[
            pltpu.VMEM((NT, NX, tok, TILE), BF),
            pltpu.VMEM((NT, NX, tok, TILE), BF),
            pltpu.VMEM((NT, NX, tok, TILE), F32),
            pltpu.VMEM((NT, 3, tok, TILE), BF),
            pltpu.VMEM((2, NT, tok // 2, TILE), BF),
            pltpu.VMEM((2, NT, tok, TILE), BF),
            pltpu.VMEM((NY, 8, 128), F32),
            pltpu.VMEM((NZ, 8, 128), F32),
            dma(NT), dma(NT), dma(2, 3, NT), dma(2, 3, NT),
            dma(NY - 1), dma(NY - 1), dma(NZ - 1), dma(NZ - 1),
        ],
        compiler_params=params(2),
        name="logits",
    )(normed, hw, jnp.pad(tgt.reshape(1, tok), ((0, 0), (0, 128 - tok))))
    return hidden, logprobs.reshape(tok)


def solution(mesh):
    placed = (
        P("seq", None),
        P("seq", None),
        P("seq", None),
        P(("seq", "vocab"), None),
        P(("seq", "vocab"), None),
        P(),
        P("seq", "vocab"),
        P("seq", "vocab"),
        P("vocab"),
        P("vocab", "seq"),
        P("vocab"),
    )
    return jax.shard_map(
        shards,
        mesh=mesh,
        in_specs=placed,
        out_specs=(P("seq", "vocab"), P("vocab")),
        check_vma=False,
    )
```

time: 839 us -> 186 us (0.22)
  waiting for transfers between devices: 432 us -> 0 us
  blocking collectives: 184 us -> 0 us
  Pallas kernels: 0 us -> 181 us
  other arithmetic: 69.1 us -> 0 us
  matrix products: 60.1 us -> 0 us
  starting transfers between devices: 35.7 us -> 0 us
  local copies, waits for them, and re-layouts: 36.9 us -> 2.88 us
  between operations: 14.1 us -> 1.32 us
    reduce_scatter x2 -> x0, waiting for transfers between devices: 249 us -> none  [the longest x1 214 us: shards(): lax.psum_scatter(jnp.dot(rows_in, out_weight, preferred_element_type=jnp....]
    pallas_call x0 -> x3, Pallas kernels: none -> 181 us  [the longest x1 87.2 us: shards(): pl.pallas_call(attention_kernel, out_shape=jax.ShapeDtypeStruct((ROWS, GW...]
    all_to_all x5 -> x0, waiting for transfers between devices: 101 us -> none  [the longest x1 44.5 us: shards(): lax.all_to_all(expand_heads(prefix_cached_values, key_value_table, HEAD_S...]
    psum x2 -> x0, blocking collectives: 86.7 us -> none  [the longest x1 74.2 us: shards(): row_total, picked = lax.psum((local_total, target_part), 'seq')]
    all_gather x2 -> x0, waiting for transfers between devices: 81.9 us -> none  [the longest x1 72.3 us: shards(): normed_all = lax.all_gather(normed, 'seq', axis=0, tiled=True)]
    pmax x1 -> x0, blocking collectives: 71.1 us -> none  [shards(): row_peak = lax.pmax(local_peak, 'seq')]
    dot_general x20 -> x0, matrix products: 60.1 us -> none  [the longest x9 30.3 us: absorb(): jnp.einsum('thk,kd->thd', weights.astype(jnp.bfloat16), values, preferred...]
    all_to_all x5 -> x0, starting transfers between devices: 35.6 us -> none  [the longest x1 11.7 us: shards(): lax.all_to_all(wide_keys, 'seq', split_axis=1, concat_axis=0, tiled=True)]
  transfers between devices with their start and end apart: 9 -> 0, of which waited for: 8 -> 0; matrix products, arithmetic and copies ran while one was open for 12% -> 0% of each run, Pallas kernels for 0% -> 0%
where the time goes in v1:
time: 186 us; the launch traced here: 185 us
  Pallas kernels  181 us (97%)
  local copies, waits for them, and re-layouts  2.88 us (2%)
    pallas_call x1, Pallas kernels, shards(): pl.pallas_call(attention_kernel, out_shape=jax.ShapeDtypeStruct((ROWS, GW...  87.2 us
    pallas_call x1, Pallas kernels, shards(): pl.pallas_call(project_kernel, out_shape=(jax.ShapeDtypeStruct((ROWS, GW)...  64.9 us
    pallas_call x1, Pallas kernels, shards(): pl.pallas_call(logits_kernel, out_shape=jax.ShapeDtypeStruct((1, tok), F3...  28.6 us

profile of v1, /device:TPU:8, one launch (start us, length us, event | category | flops | bytes accessed | tf_op | source)
XLA Modules:
  0.0 184.9 jit_solution(6055653233761667106)
XLA Ops:
  1.3 87.2 %attention.1.att_ref = bf16[16,1024]{1,0:T(8,128)(2,1)} custom-call(bf16[16,8192]{1,0:T(8,128)(2,1)} %q_ref.1, bf16[16,1024]{1,0:T(8,128)(2,1)} %sk_ref.1, bf16[16,1024]{1,0:T(8,128)(2,1)} %sv_ref.1, bf16[256,1024]{1,0:T(8,128)(2,1)} %ck_ref.1, bf16[256,1024]{1,0:T(8,128)(2,1)} %cv_ref.1, s32[1]{0:T(128)S(6)} %copy.15.start_ref), custom_call_target="tpu_custom_call" | custom-call | tf_op jit(solution)/shard_map/attention/pallas_call | solution.py:551
  88.5 64.9 %project.1 = (bf16[16,1024]{1,0:T(8,128)(2,1)}, bf16[4,8,16,1024]{3,2,1,0:T(8,128)(2,1)}) custom-call(bf16[16,1024]{1,0:T(8,128)(2,1)} %attention.1.att_ref, bf16[256,1024]{1,0:T(8,128)(2,1)} %w_ref.1, bf16[16,1024]{1,0:T(8,128)(2,1)} %res_ref.1, f32[1,1024]{1,0:T(1,128)} %bitcast.3), custom_call_target="tpu_custom_call" | custom-call | tf_op jit(solution)/shard_map/project/pallas_call | solution.py:573
  153.4 0.0 copy-start
  153.4 1.2 pad.4.tgt_ref
  154.6 28.6 %logits.1 = f32[1,64]{1,0:T(1,128)} custom-call(bf16[4,8,16,1024]{3,2,1,0:T(8,128)(2,1)} %get-tuple-element.5.n_ref, bf16[1024,2048]{1,0:T(8,128)(2,1)} %hw_ref.1, s32[1,128]{1,0:T(1,128)} %pad.4.tgt_ref), custom_call_target="tpu_custom_call" | custom-call | tf_op jit(solution)/shard_map/logits/pallas_call | solution.py:595
  183.2 0.0 copy-done
  183.2 0.6 copy.16
  183.8 1.1 copy.17
Async XLA Ops:
  153.4 29.8 %copy-start = (bf16[16,1024]{1,0:T(8,128)(2,1)S(1)}, bf16[16,1024]{1,0:T(8,128)(2,1)}, u32[]{:S(2)}) copy-start(bf16[16,1024]{1,0:T(8,128)(2,1)} %get-tuple-element.8) | copy-start | bytes 98308

commit v2 on v1

v2 whole, which is shorter than its diff:
```python
import functools
import math

import jax
import jax.numpy as jnp
from jax import lax
from jax.experimental import pallas as pl
from jax.experimental.pallas import tpu as pltpu
from jax.sharding import PartitionSpec as P

D = 8192
HEADS = 8
HS = 128
NY, NZ, NX = 4, 8, 4
NV = 2 * NX
ROWS = 16
CACHE = 256
KEYS = NV * CACHE
KEYS_PAD = KEYS + 128
GW = HEADS * HS
PW = GW + 128
VOC = 2048
TILE = 512
NT = VOC // TILE
FEAT = 256
BIG_NEG = -1e30
EPSILON = 1e-05
MESH = pl.DeviceIdType.MESH
BF = jnp.bfloat16
F32 = jnp.float32


class Place:
    def __init__(self):
        s, v = lax.axis_index("seq"), lax.axis_index("vocab")
        self.s, self.v = s, v
        self.z, self.y = lax.div(s, NY), lax.rem(s, NY)
        self.x, self.c = lax.div(v, 2), lax.rem(v, 2)

    def yy(self, d):
        return lax.rem(self.y + d + NY, NY)

    def zz(self, d):
        return lax.rem(self.z + d + NZ, NZ)

    def xx(self, d):
        return lax.rem(self.x + d + NX, NX)

    def at_z(self, d):
        return (self.zz(d) * NY + self.y, self.v)

    def at_y(self, d):
        return (self.z * NY + self.yy(d), self.v)

    def at_x(self, d, core):
        return (self.s, self.xx(d) * 2 + core)

    def at_v(self, d):
        return (self.s, lax.rem(self.v + d, NV))


def rdma(src, dst, send, recv, dev):
    return pltpu.make_async_remote_copy(
        src_ref=src, dst_ref=dst, send_sem=send, recv_sem=recv, device_id=dev, device_id_type=MESH
    )


def greet(partners):
    bar = pltpu.get_barrier_semaphore()
    for dev in partners:
        pl.semaphore_signal(bar, inc=1, device_id=dev, device_id_type=MESH)
    pl.semaphore_wait(bar, len(partners))


def gather_start(me, go, buf, zs, zr):
    own = buf.at[me.y, me.z]
    for d in (1, 7, 2, 6, 3, 5, 4):
        go(rdma(own, own, zs.at[d - 1], zr.at[d - 1], me.at_z(d)))


def gather_seq(me, go, buf, zs, zr, ys, yr):
    for d in (0, 1, 7, 2, 6, 3, 5, 4):
        blk = buf.at[me.y, me.zz(-d)]
        if d:
            rdma(blk, blk, zs.at[d - 1], zr.at[d - 1], me.at_z(1)).wait_recv()
        for e in (2, 1, 3):
            go(rdma(blk, blk, ys.at[e - 1, d], yr.at[e - 1, d], me.at_y(e)))


def gather_wait(me, buf, ys, yr):
    for e in (2, 1, 3):
        for d in range(NZ):
            blk = buf.at[me.yy(-e), me.zz(-d)]
            rdma(blk, blk, ys.at[e - 1, d], yr.at[e - 1, d], me.at_y(e)).wait_recv()


def ring_step(me, go, step, buf, ss, rs):
    rows = buf.shape[1]
    for k, way in ((0, 1), (1, -1)):
        if step == 1:
            blk = buf.at[me.z]
        else:
            blk = buf.at[me.zz(-way * (step - 1))]
            rdma(blk, blk, ss.at[k, step - 2], rs.at[k, step - 2], me.at_z(way)).wait_recv()
        if step == NZ // 2:
            blk = buf.at[me.zz(-way * (step - 1)), pl.ds(k * (rows // 2), rows // 2)]
        go(rdma(blk, blk, ss.at[k, step - 1], rs.at[k, step - 1], me.at_z(way)))


def ring_wait(me, buf, ss, rs):
    rows = buf.shape[1]
    step = NZ // 2
    for k, way in ((0, 1), (1, -1)):
        blk = buf.at[me.zz(step), pl.ds(k * (rows // 2), rows // 2)]
        rdma(blk, blk, ss.at[k, step - 1], rs.at[k, step - 1], me.at_z(way)).wait_recv()


def lanes(shape):
    return lax.broadcasted_iota(jnp.int32, shape, len(shape) - 1)


def pack_lse(lse, low8):
    second = pltpu.roll(lse, 8, 1) if low8 else lse
    third = pltpu.roll(lse, 16, 1) if low8 else lse

    def split(a):
        hi = a.astype(BF).astype(F32)
        mid = (a - hi).astype(BF).astype(F32)
        return hi, mid, a - hi - mid

    lane = lanes(lse.shape)
    out = jnp.where(lane < 8, split(lse)[0], jnp.where(lane < 16, split(second)[1], split(third)[2]))
    return jnp.where(lane < 24, out, 0.0).astype(BF)


def unpack_lse(packed):
    a = packed.astype(F32)
    return a + (pltpu.roll(a, 120, 1) + pltpu.roll(a, 112, 1))


def join_partials(items, final=False):
    lses = [unpack_lse(it[:, GW:]) for it in items]
    peak = functools.reduce(jnp.maximum, lses)
    weights = [jnp.exp2(l - peak) for l in lses]
    total = functools.reduce(jnp.add, weights)
    weights = [w / total for w in weights]
    cols = []
    for h in range(HEADS):
        acc = None
        for w, it in zip(weights, items):
            term = w[:, h : h + 1] * it[:, h * HS : (h + 1) * HS].astype(F32)
            acc = term if acc is None else acc + term
        cols.append(acc.astype(BF))
    if not final:
        cols.append(pack_lse(peak + jnp.log2(total), True))
    return jnp.concatenate(cols, axis=1)


def kernel(
    q_ref, sk_ref, sv_ref, ck_ref, cv_ref, start_ref, w_ref, res_ref, gain_ref, hw_hbm, tgt_ref,
    hid_ref, out_ref,
    qall, kbuf, vbuf, vext, bias, lse_buf, opart, ry, mg, rz, wall, hw_ref, tin, aall, ppart, rp, sq, nall,
    osend, orecv, own, sx, x2, sty, stz,
    loc, kvs, kr, vr, gz, gzr, gy, gyr, ws, wr, rys, ryr, rzs, rzr, tss, trs, avs, avr, ps_, pr_, sqs, sqr,
    hz, hzr, hy, hyr, cs, cr, xs, xr, yss, yrs, zss, zrs,
):
    me = Place()
    sends = []

    def go(cp):
        cp.start()
        sends.append(cp)

    def cols(vv):
        return pl.ds(pl.multiple_of(vv * HS, HS), HS)

    def rows(vv):
        return pl.ds(pl.multiple_of(vv * CACHE, CACHE), CACHE)

    head_cols = pl.ds(pl.multiple_of(me.v * GW, GW), GW)
    own_q = pltpu.make_async_copy(q_ref.at[:, head_cols], qall.at[me.y, me.z], loc.at[0])
    own_q.start()
    own_w = pltpu.make_async_copy(w_ref, wall.at[me.z], loc.at[1])
    own_w.start()
    own_k = pltpu.make_async_copy(ck_ref.at[:, cols(me.v)], kbuf.at[rows(me.v)], kr.at[me.v])
    own_v = pltpu.make_async_copy(cv_ref.at[:, cols(me.v)], vbuf.at[rows(me.v)], vr.at[me.v])
    own_k.start()
    own_v.start()
    own_hw = pltpu.make_async_copy(hw_hbm, hw_ref, loc.at[2])
    own_hw.start()
    kbuf[KEYS:, :] = jnp.zeros((128, HS), BF)
    vbuf[KEYS:, :] = jnp.zeros((128, HS), BF)
    kbuf[KEYS : KEYS + ROWS, :] = sk_ref[:, cols(me.v)]
    vbuf[KEYS : KEYS + ROWS, :] = sv_ref[:, cols(me.v)]
    flat = lanes((1, KEYS_PAD))
    bias[...] = jnp.where(flat < start_ref[0] - me.s * KEYS, 0.0, BIG_NEG)
    own_q.wait()
    greet(
        [me.at_z(d) for d in range(1, NZ)]
        + [me.at_y(d) for d in range(1, NY)]
        + [me.at_v(d) for d in range(1, NV)]
    )

    gather_start(me, go, qall, gz, gzr)
    for i, d in enumerate((4, 3, 5, 2, 6, 1, 7)):
        vv = lax.rem(me.v + d, NV)
        go(rdma(ck_ref.at[:, cols(vv)], kbuf.at[rows(me.v)], kvs.at[0, i], kr.at[me.v], me.at_v(d)))
        go(rdma(cv_ref.at[:, cols(vv)], vbuf.at[rows(me.v)], kvs.at[1, i], vr.at[me.v], me.at_v(d)))
    gather_seq(me, go, qall, gz, gzr, gy, gyr)
    own_w.wait()
    ring_step(me, go, 1, wall, ws, wr)
    own_k.wait()
    own_v.wait()
    for d in range(1, NV):
        src = lax.rem(me.v + d, NV)
        blk = kbuf.at[rows(src)]
        rdma(blk, blk, kvs.at[0, 0], kr.at[src], me.at_v(1)).wait_recv()
        blk = vbuf.at[rows(src)]
        rdma(blk, blk, kvs.at[1, 0], vr.at[src], me.at_v(1)).wait_recv()
    vext[:, :HS] = vbuf[...]
    vext[:, HS:] = jnp.ones((KEYS_PAD, HS), BF)
    gather_wait(me, qall, gy, gyr)

    scale = math.log2(math.e) / math.sqrt(HS)
    nrow = NZ * ROWS
    for turn, order in enumerate((2, 1, 3, 0)):
        yy = me.yy(order)
        if turn:
            ring_step(me, go, turn + 1, wall, ws, wr)

        def pair(hp, carry):
            both = []
            for i in range(2):
                at = pl.ds(pl.multiple_of((hp * 2 + i) * HS, HS), HS)
                both.append(qall[yy, :, :, at].reshape(nrow, HS))
            q2 = jnp.concatenate(both, axis=0)
            sc = lax.dot_general(q2, kbuf[...], (((1,), (1,)), ((), ())), preferred_element_type=F32)
            main = sc[:, :KEYS] * scale + bias[:, :KEYS]
            row = lax.broadcasted_iota(jnp.int32, (2 * nrow, 128), 0)
            row = lax.rem(row, nrow)
            token = lax.div(row, ROWS) * (NY * ROWS) + yy * ROWS + lax.rem(row, ROWS)
            key = lanes((2 * nrow, 128))
            ok = (key < ROWS) & (key + me.s * ROWS <= token)
            span = jnp.where(ok, sc[:, KEYS:] * scale, BIG_NEG)
            peak = jnp.maximum(
                jnp.max(main, axis=1, keepdims=True), jnp.max(span, axis=1, keepdims=True)
            )
            pm = jnp.exp2(main - peak).astype(BF)
            ps = jnp.exp2(span - peak).astype(BF)
            ps = jnp.where(ok, ps, jnp.zeros_like(ps))
            o = jnp.dot(pm, vext[:KEYS, :], preferred_element_type=F32)
            o = o + jnp.dot(ps, vext[KEYS:, :], preferred_element_type=F32)
            total = o[:, HS:]
            total = jnp.where(total > 0.0, total, 1.0)
            on = (o[:, :HS] / total).astype(BF)
            lse = peak + jnp.log2(total)
            lane = lanes((nrow, 128))
            for i in range(2):
                h = hp * 2 + i
                at = pl.ds(pl.multiple_of(h * HS, HS), HS)
                opart[yy, :, :, at] = on[i * nrow : (i + 1) * nrow].reshape(NZ, ROWS, HS)
                mine = lse[i * nrow : (i + 1) * nrow]
                lse_buf[...] = jnp.where(lax.rem(lane, 8) == h, mine, lse_buf[...])
            return carry

        lax.fori_loop(0, HEADS // 2, pair, 0)
        opart[yy, :, :, GW:] = pack_lse(lse_buf[...], False).reshape(NZ, ROWS, 128)
        if order:
            go(rdma(opart.at[yy], ry.at[order - 1], rys.at[order - 1], ryr.at[order - 1], me.at_y(order)))

    items = [opart[me.y].reshape(nrow, PW)]
    for d in (2, 1, 3):
        blk = ry.at[d - 1]
        rdma(blk, blk, rys.at[d - 1], ryr.at[d - 1], me.at_y(d)).wait_recv()
        items.append(ry[d - 1].reshape(nrow, PW))
    mg[...] = join_partials(items).reshape(NZ, ROWS, PW)
    for d in (4, 3, 5, 2, 6, 1, 7):
        go(rdma(mg.at[me.zz(d)], rz.at[d - 1], rzs.at[d - 1], rzr.at[d - 1], me.at_z(d)))
    items = [mg[me.z]]
    for d in range(1, NZ):
        blk = rz.at[d - 1]
        rdma(blk, blk, rzs.at[d - 1], rzr.at[d - 1], me.at_z(d)).wait_recv()
        items.append(rz[d - 1])
    att = join_partials(items, final=True)

    for j in range(NY):
        tin[0, j] = att[:, j * FEAT : (j + 1) * FEAT]
    aall[me.v, me.y] = tin[0, me.y]
    for d in (2, 1, 3):
        go(rdma(tin.at[0, me.yy(d)], aall.at[me.v, me.y], tss.at[d - 1], trs.at[d - 1], me.at_y(d)))
    for d in (2, 1, 3):
        blk = aall.at[me.v, me.yy(-d)]
        rdma(blk, blk, tss.at[d - 1], trs.at[d - 1], me.at_y(d)).wait_recv()
    for d in (4, 3, 5, 2, 6, 1, 7):
        blk = aall.at[me.v]
        go(rdma(blk, blk, avs.at[d - 1], avr.at[d - 1], me.at_v(d)))
    ring_wait(me, wall, ws, wr)
    tok = NY * ROWS
    proj = jnp.dot(aall[me.v].reshape(tok, FEAT), wall[me.v], preferred_element_type=F32)
    for d in (1, 7, 2, 6, 3, 5, 4):
        src = lax.rem(me.v - d + NV, NV)
        blk = aall.at[src]
        rdma(blk, blk, avs.at[d - 1], avr.at[d - 1], me.at_v(1)).wait_recv()
        proj = proj + jnp.dot(aall[src].reshape(tok, FEAT), wall[src], preferred_element_type=F32)
    ppart[...] = proj.astype(BF).reshape(NY, ROWS, GW)
    for d in (2, 1, 3):
        go(rdma(ppart.at[me.yy(d)], rp.at[d - 1], ps_.at[d - 1], pr_.at[d - 1], me.at_y(d)))
    total = res_ref[...].astype(F32) + ppart[me.y].astype(F32)
    for d in (1, 3, 2):
        blk = rp.at[d - 1]
        rdma(blk, blk, ps_.at[d - 1], pr_.at[d - 1], me.at_y(d)).wait_recv()
        total = total + rp[d - 1].astype(F32)
    hidden = total.astype(BF)
    hid_ref[...] = hidden

    wide = hidden.astype(F32)
    sq[me.v] = jnp.broadcast_to(jnp.sum(wide * wide, axis=1, keepdims=True), (ROWS, 128))
    for d in (4, 3, 5, 2, 6, 1, 7):
        go(rdma(sq.at[me.v], sq.at[me.v], sqs.at[d - 1], sqr.at[d - 1], me.at_v(d)))
    for d in range(1, NV):
        blk = sq.at[lax.rem(me.v - d + NV, NV)]
        rdma(blk, blk, sqs.at[d - 1], sqr.at[d - 1], me.at_v(1)).wait_recv()
    mean = jnp.sum(sq[...], axis=0)[:, :1] * (1.0 / D)
    nall[me.y, me.z] = (wide * lax.rsqrt(mean + EPSILON) * gain_ref[...]).astype(BF)
    gather_start(me, go, nall, hz, hzr)
    gather_seq(me, go, nall, hz, hzr, hy, hyr)
    own_hw.wait()
    gather_wait(me, nall, hy, hyr)

    shift = (2, 1, 3, 0)

    def rows_of(core):
        blocks = []
        for d in shift:
            for y in range(NY):
                blocks.append(nall[y, me.xx(d) * 2 + core])
        return jnp.concatenate(blocks, axis=0)

    sib = me.at_x(0, 1 - me.c)
    lhs = rows_of(1 - me.c)
    for n in range(NT):
        at = pl.ds(n * TILE, TILE)
        osend[n] = (
            jnp.dot(lhs, hw_ref[:, at], preferred_element_type=F32).astype(BF).reshape(NX, tok, TILE)
        )
        go(rdma(osend.at[n], orecv.at[n], cs.at[n], cr.at[n], sib))
    lhs = rows_of(me.c)
    for n in range(NT):
        at = pl.ds(n * TILE, TILE)
        mine = jnp.dot(lhs, hw_ref[:, at], preferred_element_type=F32).reshape(NX, tok, TILE)
        rdma(orecv.at[n], orecv.at[n], cs.at[n], cr.at[n], sib).wait_recv()
        mine = mine + orecv[n].astype(F32)
        own[n] = mine[3]
        sx[n] = mine[:3].astype(BF)
        for i, d in enumerate(shift[:3]):
            go(rdma(sx.at[n, i], x2.at[n, i], xs.at[n, i], xr.at[n, i], me.at_x(d, me.c)))

    tgt = jnp.concatenate([tgt_ref[...], jnp.zeros((1, 128 - tok), jnp.int32)], axis=1)
    tgt = jnp.broadcast_to(tgt.astype(F32), (128, 128))
    tgt = jnp.transpose(tgt)[:tok, :1].astype(jnp.int32) - me.s * VOC
    peak = None
    for n in range(NT):
        lg = own[n]
        for i, d in enumerate(shift[:3]):
            blk = x2.at[n, i]
            rdma(blk, blk, xs.at[n, i], xr.at[n, i], me.at_x(d, me.c)).wait_recv()
            lg = lg + x2[n, i].astype(F32)
        own[n] = lg
        top = jnp.max(lg, axis=1, keepdims=True)
        peak = top if peak is None else jnp.maximum(peak, top)
    total = picked = None
    for n in range(NT):
        lg = own[n]
        a = jnp.sum(jnp.exp(lg - peak), axis=1, keepdims=True)
        b = jnp.sum(jnp.where(lanes((tok, TILE)) + n * TILE == tgt, lg, 0.0), axis=1, keepdims=True)
        total = a if total is None else total + a
        picked = b if picked is None else picked + b
    lane = lanes((tok, 128))
    st = jnp.where(lane == 0, peak, jnp.where(lane == 1, total, picked))
    st = jnp.concatenate([st, jnp.zeros((128 - tok, 128), F32)], axis=0)
    sty[0] = jnp.transpose(st)[:8]

    def joined(buf, count):
        top = functools.reduce(jnp.maximum, [buf[i, 0:1] for i in range(count)])
        tot = functools.reduce(jnp.add, [buf[i, 1:2] * jnp.exp(buf[i, 0:1] - top) for i in range(count)])
        pick = functools.reduce(jnp.add, [buf[i, 2:3] for i in range(count)])
        return top, tot, pick

    for d in (2, 1, 3):
        go(rdma(sty.at[0], sty.at[d], yss.at[d - 1], yrs.at[d - 1], me.at_y(d)))
    for d in range(1, NY):
        rdma(sty.at[d], sty.at[d], yss.at[d - 1], yrs.at[d - 1], me.at_y(d)).wait_recv()
    top, tot, pick = joined(sty, NY)
    stz[0] = jnp.concatenate([top, tot, pick, jnp.zeros((5, 128), F32)], axis=0)
    for d in (4, 3, 5, 2, 6, 1, 7):
        go(rdma(stz.at[0], stz.at[d], zss.at[d - 1], zrs.at[d - 1], me.at_z(d)))
    for d in range(1, NZ):
        rdma(stz.at[d], stz.at[d], zss.at[d - 1], zrs.at[d - 1], me.at_z(d)).wait_recv()
    top, tot, pick = joined(stz, NZ)
    out_ref[...] = (pick - (top + jnp.log(tot)))[:, :tok]
    for cp in sends:
        cp.wait_send()


def vm():
    return pl.BlockSpec(memory_space=pltpu.VMEM)


def params(cid):
    return pltpu.CompilerParams(
        collective_id=cid, has_side_effects=True, vmem_limit_bytes=56 * 1024 * 1024
    )


def dma(*shape):
    return pltpu.SemaphoreType.DMA(shape)


def shards(q, sk, sv, ck, cv, start, w, res, gain, hw, tgt):
    any_ = pl.BlockSpec(memory_space=pl.ANY)
    tok = NY * ROWS
    hidden, logprobs = pl.pallas_call(
        kernel,
        out_shape=(
            jax.ShapeDtypeStruct((ROWS, GW), BF),
            jax.ShapeDtypeStruct((1, tok), F32),
        ),
        in_specs=[any_, vm(), vm(), any_, any_, pl.BlockSpec(memory_space=pltpu.SMEM)]
        + [any_, vm(), vm(), any_, vm()],
        out_specs=(vm(), vm()),
        scratch_shapes=[
            pltpu.VMEM((NY, NZ, ROWS, GW), BF),
            pltpu.VMEM((KEYS_PAD, HS), BF),
            pltpu.VMEM((KEYS_PAD, HS), BF),
            pltpu.VMEM((KEYS_PAD, 2 * HS), BF),
            pltpu.VMEM((1, KEYS_PAD), F32),
            pltpu.VMEM((NZ * ROWS, 128), F32),
            pltpu.VMEM((NY, NZ, ROWS, PW), BF),
            pltpu.VMEM((NY - 1, NZ, ROWS, PW), BF),
            pltpu.VMEM((NZ, ROWS, PW), BF),
            pltpu.VMEM((NZ - 1, ROWS, PW), BF),
            pltpu.VMEM((NZ, FEAT, GW), BF),
            pltpu.VMEM((GW, VOC), BF),
            pltpu.VMEM((1, NY, ROWS, FEAT), BF),
            pltpu.VMEM((NV, NY, ROWS, FEAT), BF),
            pltpu.VMEM((NY, ROWS, GW), BF),
            pltpu.VMEM((NY - 1, ROWS, GW), BF),
            pltpu.VMEM((NV, ROWS, 128), F32),
            pltpu.VMEM((NY, NZ, ROWS, GW), BF),
            pltpu.VMEM((NT, NX, tok, TILE), BF),
            pltpu.VMEM((NT, NX, tok, TILE), BF),
            pltpu.VMEM((NT, tok, TILE), F32),
            pltpu.VMEM((NT, NX - 1, tok, TILE), BF),
            pltpu.VMEM((NT, NX - 1, tok, TILE), BF),
            pltpu.VMEM((NY, 8, 128), F32),
            pltpu.VMEM((NZ, 8, 128), F32),
            dma(3), dma(2, NV - 1), dma(NV), dma(NV),
            dma(NZ - 1), dma(NZ - 1), dma(NY - 1, NZ), dma(NY - 1, NZ),
            dma(2, NZ // 2), dma(2, NZ // 2),
            dma(NY - 1), dma(NY - 1), dma(NZ - 1), dma(NZ - 1),
            dma(NY - 1), dma(NY - 1), dma(NV - 1), dma(NV - 1),
            dma(NY - 1), dma(NY - 1), dma(NV - 1), dma(NV - 1),
            dma(NZ - 1), dma(NZ - 1), dma(NY - 1, NZ), dma(NY - 1, NZ),
            dma(NT), dma(NT), dma(NT, NX - 1), dma(NT, NX - 1),
            dma(NY - 1), dma(NY - 1), dma(NZ - 1), dma(NZ - 1),
        ],
        compiler_params=params(0),
        name="layer",
    )(q, sk, sv, ck, cv, start, w, res, gain.reshape(1, GW), hw, tgt.reshape(1, tok))
    return hidden, logprobs.reshape(tok)


def solution(mesh):
    placed = (
        P("seq", None),
        P("seq", None),
        P("seq", None),
        P(("seq", "vocab"), None),
        P(("seq", "vocab"), None),
        P(),
        P("seq", "vocab"),
        P("seq", "vocab"),
        P("vocab"),
        P("vocab", "seq"),
        P("vocab"),
    )
    return jax.shard_map(
        shards,
        mesh=mesh,
        in_specs=placed,
        out_specs=(P("seq", "vocab"), P("vocab")),
        check_vma=False,
    )
```

time: 186 us -> 134 us (0.72)
  Pallas kernels: 181 us -> 130 us
    pallas_call x3 -> x1, Pallas kernels: 181 us -> 130 us  [shards(): pl.pallas_call(kernel, out_shape=(jax.ShapeDtypeStruct((ROWS, GW), BF), j...]
where the time goes in v2:
time: 134 us; the launch traced here: 133 us
  Pallas kernels  130 us (97%)
  local copies, waits for them, and re-layouts  2.55 us (2%)
    pallas_call x1, Pallas kernels, shards(): pl.pallas_call(kernel, out_shape=(jax.ShapeDtypeStruct((ROWS, GW), BF), j...  130 us

profile of v2, /device:TPU:8, one launch (start us, length us, event | category | flops | bytes accessed | tf_op | source)
XLA Modules:
  0.0 133.4 jit_solution(895424819024271299)
XLA Ops:
  1.3 129.6 %layer.1 = (bf16[16,1024]{1,0:T(8,128)(2,1)}, f32[1,64]{1,0:T(1,128)}) custom-call(bf16[16,8192]{1,0:T(8,128)(2,1)} %q_ref.1, bf16[16,1024]{1,0:T(8,128)(2,1)} %sk_ref.1, bf16[16,1024]{1,0:T(8,128)(2,1)} %sv_ref.1, bf16[256,1024]{1,0:T(8,128)(2,1)} %ck_ref.1, bf16[256,1024]{1,0:T(8,128)(2,1)} %cv_ref.1, s32[1]{0:T(128)S(6)} %copy.15.start_ref, ...), custom_call_target="tpu_custom_call" | custom-call | tf_op jit(solution)/shard_map/layer/pallas_call | solution.py:422
  130.9 1.4 %copy.16 = bf16[16,1024]{1,0:T(8,128)(2,1)} copy(bf16[16,1024]{1,0:T(8,128)(2,1)} %get-tuple-element.8) | data formatting | bytes 65536
  132.3 1.2 copy.17

commit v3 on v2

--- a/solution.py
+++ b/solution.py
@@ -69,50 +69,58 @@
     bar = pltpu.get_barrier_semaphore()
     for dev in partners:
         pl.semaphore_signal(bar, inc=1, device_id=dev, device_id_type=MESH)
-    pl.semaphore_wait(bar, len(partners))
 
 
 def gather_start(me, go, buf, zs, zr):
     own = buf.at[me.y, me.z]
     for d in (1, 7, 2, 6, 3, 5, 4):
-        go(rdma(own, own, zs.at[d - 1], zr.at[d - 1], me.at_z(d)))
-
-
-def gather_seq(me, go, buf, zs, zr, ys, yr):
-    for d in (0, 1, 7, 2, 6, 3, 5, 4):
-        blk = buf.at[me.y, me.zz(-d)]
-        if d:
-            rdma(blk, blk, zs.at[d - 1], zr.at[d - 1], me.at_z(1)).wait_recv()
-        for e in (2, 1, 3):
-            go(rdma(blk, blk, ys.at[e - 1, d], yr.at[e - 1, d], me.at_y(e)))
-
-
-def gather_wait(me, buf, ys, yr):
+        go(rdma(own, own, zs.at[d - 1], zr.at[me.z], me.at_z(d)))
+
+
+def gather_pass(me, go, buf, src, own, zs, zr, ys, yr):
+    blk = buf.at[me.y, src]
+    if not own:
+        rdma(blk, blk, zs.at[0], zr.at[src], me.at_z(1)).wait_recv()
     for e in (2, 1, 3):
-        for d in range(NZ):
-            blk = buf.at[me.yy(-e), me.zz(-d)]
-            rdma(blk, blk, ys.at[e - 1, d], yr.at[e - 1, d], me.at_y(e)).wait_recv()
-
-
-def ring_step(me, go, step, buf, ss, rs):
-    rows = buf.shape[1]
+        go(rdma(blk, blk, ys.at[e - 1, src], yr.at[e - 1, src], me.at_y(e)))
+
+
+def gather_wait(me, buf, e, src, ys, yr):
+    blk = buf.at[me.yy(-e), src]
+    rdma(blk, blk, ys.at[e - 1, src], yr.at[e - 1, src], me.at_y(e)).wait_recv()
+
+
+PIECES = 4
+TICKS = [(step, p) for step in range(NZ // 2 - 1) for p in range(PIECES)]
+TICKS += [(NZ // 2 - 1, p) for p in range(PIECES // 2)]
+
+
+def ring_piece(me, buf, k, way, step, p):
+    rows = buf.shape[1] // PIECES
+    p = p + k * (PIECES // 2) if step == NZ // 2 - 1 else p
+    return buf.at[me.zz(-way * step), pl.ds(p * rows, rows)], p
+
+
+def ring_tick(me, go, tick, buf, ss, rs):
+    step, p0 = TICKS[tick]
     for k, way in ((0, 1), (1, -1)):
-        if step == 1:
-            blk = buf.at[me.z]
-        else:
-            blk = buf.at[me.zz(-way * (step - 1))]
-            rdma(blk, blk, ss.at[k, step - 2], rs.at[k, step - 2], me.at_z(way)).wait_recv()
-        if step == NZ // 2:
-            blk = buf.at[me.zz(-way * (step - 1)), pl.ds(k * (rows // 2), rows // 2)]
-        go(rdma(blk, blk, ss.at[k, step - 1], rs.at[k, step - 1], me.at_z(way)))
+        blk, p = ring_piece(me, buf, k, way, step, p0)
+        if step:
+            rdma(blk, blk, ss.at[k, 0], rs.at[k, (step - 1) * PIECES + p], me.at_z(way)).wait_recv()
+        go(rdma(blk, blk, ss.at[k, tick], rs.at[k, step * PIECES + p], me.at_z(way)))
 
 
 def ring_wait(me, buf, ss, rs):
-    rows = buf.shape[1]
-    step = NZ // 2
+    last = NZ // 2 - 1
+    rows = buf.shape[1] // PIECES
     for k, way in ((0, 1), (1, -1)):
-        blk = buf.at[me.zz(step), pl.ds(k * (rows // 2), rows // 2)]
-        rdma(blk, blk, ss.at[k, step - 1], rs.at[k, step - 1], me.at_z(way)).wait_recv()
+        for p in range(PIECES):
+            if p // (PIECES // 2) == k:
+                blk = buf.at[me.zz(-way * (last + 1)), pl.ds(p * rows, rows)]
+                rdma(blk, blk, ss.at[k, 0], rs.at[k, last * PIECES + p], me.at_z(way)).wait_recv()
+            else:
+                blk = buf.at[me.zz(-way * last), pl.ds(p * rows, rows)]
+                rdma(blk, blk, ss.at[k, 0], rs.at[k, (last - 1) * PIECES + p], me.at_z(way)).wait_recv()
 
 
 def lanes(shape):
@@ -157,11 +165,11 @@
 
 
 def kernel(
-    q_ref, sk_ref, sv_ref, ck_ref, cv_ref, start_ref, w_ref, res_ref, gain_ref, hw_hbm, tgt_ref,
+    q_ref, sk_ref, sv_ref, ck_ref, cv_ref, start_ref, w_ref, res_hbm, gain_hbm, hw_hbm, tgt_hbm,
     hid_ref, out_ref,
-    qall, kbuf, vbuf, vext, bias, lse_buf, opart, ry, mg, rz, wall, hw_ref, tin, aall, ppart, rp, sq, nall,
-    osend, orecv, own, sx, x2, sty, stz,
-    loc, kvs, kr, vr, gz, gzr, gy, gyr, ws, wr, rys, ryr, rzs, rzr, tss, trs, avs, avr, ps_, pr_, sqs, sqr,
+    qall, kbuf, vbuf, vext, bias, lse_buf, opart, ry, mg, rz, wall, hw_ref, res_ref, gain_ref, tgt_ref, tin, aall, ppart, rp, sq, nall,
+    osend, orecv, own, final, sx, x2, sty, stz,
+    loc, kvs, kr, vr, gz, gzr, gy, gyr, ws, wr, rys, ryr, rzs, rzr, avs, avr, ps_, pr_, sqs, sqr,
     hz, hzr, hy, hyr, cs, cr, xs, xr, yss, yrs, zss, zrs,
 ):
     me = Place()
@@ -177,38 +185,51 @@
     def rows(vv):
         return pl.ds(pl.multiple_of(vv * CACHE, CACHE), CACHE)
 
+    greet(
+        [me.at_z(d) for d in range(1, NZ)]
+        + [
+            (me.z * NY + me.yy(dy), lax.rem(me.v + dv, NV))
+            for dy in range(NY)
+            for dv in range(NV)
+            if dy or dv
+        ]
+    )
+
+    def fetch(src, dst, sem):
+        cp = pltpu.make_async_copy(src, dst, sem)
+        cp.start()
+        return cp
+
     head_cols = pl.ds(pl.multiple_of(me.v * GW, GW), GW)
-    own_q = pltpu.make_async_copy(q_ref.at[:, head_cols], qall.at[me.y, me.z], loc.at[0])
-    own_q.start()
-    own_w = pltpu.make_async_copy(w_ref, wall.at[me.z], loc.at[1])
-    own_w.start()
-    own_k = pltpu.make_async_copy(ck_ref.at[:, cols(me.v)], kbuf.at[rows(me.v)], kr.at[me.v])
-    own_v = pltpu.make_async_copy(cv_ref.at[:, cols(me.v)], vbuf.at[rows(me.v)], vr.at[me.v])
-    own_k.start()
-    own_v.start()
-    own_hw = pltpu.make_async_copy(hw_hbm, hw_ref, loc.at[2])
-    own_hw.start()
-    kbuf[KEYS:, :] = jnp.zeros((128, HS), BF)
-    vbuf[KEYS:, :] = jnp.zeros((128, HS), BF)
-    kbuf[KEYS : KEYS + ROWS, :] = sk_ref[:, cols(me.v)]
-    vbuf[KEYS : KEYS + ROWS, :] = sv_ref[:, cols(me.v)]
+    own_q = fetch(q_ref.at[:, head_cols], qall.at[me.y, me.z], loc.at[0])
+    own_w = fetch(w_ref, wall.at[me.z], loc.at[1])
+    own_k = fetch(ck_ref.at[:, cols(me.v)], kbuf.at[rows(me.v)], kr.at[me.v])
+    own_v = fetch(cv_ref.at[:, cols(me.v)], vbuf.at[rows(me.v)], vr.at[me.v])
+    span_k = fetch(sk_ref.at[:, cols(me.v)], kbuf.at[pl.ds(KEYS, ROWS)], loc.at[3])
+    span_v = fetch(sv_ref.at[:, cols(me.v)], vbuf.at[pl.ds(KEYS, ROWS)], loc.at[4])
+    later = [fetch(hw_hbm, hw_ref, loc.at[2]), fetch(res_hbm, res_ref, loc.at[5])]
+    later += [fetch(gain_hbm, gain_ref, loc.at[6]), fetch(tgt_hbm, tgt_ref, loc.at[7])]
+    kbuf[KEYS + ROWS :, :] = jnp.zeros((128 - ROWS, HS), BF)
+    vbuf[KEYS + ROWS :, :] = jnp.zeros((128 - ROWS, HS), BF)
     flat = lanes((1, KEYS_PAD))
     bias[...] = jnp.where(flat < start_ref[0] - me.s * KEYS, 0.0, BIG_NEG)
     own_q.wait()
-    greet(
-        [me.at_z(d) for d in range(1, NZ)]
-        + [me.at_y(d) for d in range(1, NY)]
-        + [me.at_v(d) for d in range(1, NV)]
-    )
+    own_w.wait()
+    pl.semaphore_wait(pltpu.get_barrier_semaphore(), NZ - 1 + NY * NV - 1)
 
     gather_start(me, go, qall, gz, gzr)
     for i, d in enumerate((4, 3, 5, 2, 6, 1, 7)):
         vv = lax.rem(me.v + d, NV)
         go(rdma(ck_ref.at[:, cols(vv)], kbuf.at[rows(me.v)], kvs.at[0, i], kr.at[me.v], me.at_v(d)))
         go(rdma(cv_ref.at[:, cols(vv)], vbuf.at[rows(me.v)], kvs.at[1, i], vr.at[me.v], me.at_v(d)))
-    gather_seq(me, go, qall, gz, gzr, gy, gyr)
-    own_w.wait()
-    ring_step(me, go, 1, wall, ws, wr)
+    ring_tick(me, go, 0, wall, ws, wr)
+    ring_tick(me, go, 1, wall, ws, wr)
+    for d in (0, 1, 7, 2, 6, 3, 5, 4):
+        gather_pass(me, go, qall, me.zz(d), d == 0, gz, gzr, gy, gyr)
+    ring_tick(me, go, 2, wall, ws, wr)
+    ring_tick(me, go, 3, wall, ws, wr)
+    span_k.wait()
+    span_v.wait()
     own_k.wait()
     own_v.wait()
     for d in range(1, NV):
@@ -219,19 +240,20 @@
         rdma(blk, blk, kvs.at[1, 0], vr.at[src], me.at_v(1)).wait_recv()
     vext[:, :HS] = vbuf[...]
     vext[:, HS:] = jnp.ones((KEYS_PAD, HS), BF)
-    gather_wait(me, qall, gy, gyr)
+    ring_tick(me, go, 4, wall, ws, wr)
 
     scale = math.log2(math.e) / math.sqrt(HS)
     nrow = NZ * ROWS
     for turn, order in enumerate((2, 1, 3, 0)):
         yy = me.yy(order)
-        if turn:
-            ring_step(me, go, turn + 1, wall, ws, wr)
-
-        def pair(hp, carry):
+        if order:
+            for d in (0, 1, 7, 2, 6, 3, 5, 4):
+                gather_wait(me, qall, NY - order, me.zz(d), gy, gyr)
+
+        def pair(hp):
             both = []
             for i in range(2):
-                at = pl.ds(pl.multiple_of((hp * 2 + i) * HS, HS), HS)
+                at = pl.ds((hp * 2 + i) * HS, HS)
                 both.append(qall[yy, :, :, at].reshape(nrow, HS))
             q2 = jnp.concatenate(both, axis=0)
             sc = lax.dot_general(q2, kbuf[...], (((1,), (1,)), ((), ())), preferred_element_type=F32)
@@ -257,54 +279,67 @@
             lane = lanes((nrow, 128))
             for i in range(2):
                 h = hp * 2 + i
-                at = pl.ds(pl.multiple_of(h * HS, HS), HS)
+                at = pl.ds(h * HS, HS)
                 opart[yy, :, :, at] = on[i * nrow : (i + 1) * nrow].reshape(NZ, ROWS, HS)
                 mine = lse[i * nrow : (i + 1) * nrow]
                 lse_buf[...] = jnp.where(lax.rem(lane, 8) == h, mine, lse_buf[...])
-            return carry
-
-        lax.fori_loop(0, HEADS // 2, pair, 0)
+
+        def ship(part):
+            at = pl.ds(0, GW // 2) if part == 0 else pl.ds(GW // 2, PW - GW // 2)
+            src, dst = opart.at[yy, :, :, at], ry.at[order - 1, :, :, at]
+            go(rdma(src, dst, rys.at[part, order - 1], ryr.at[part, order - 1], me.at_y(order)))
+
+        pair(0)
+        pair(1)
+        if order:
+            ship(0)
+        ring_tick(me, go, 5 + turn, wall, ws, wr)
+        pair(2)
+        pair(3)
         opart[yy, :, :, GW:] = pack_lse(lse_buf[...], False).reshape(NZ, ROWS, 128)
         if order:
-            go(rdma(opart.at[yy], ry.at[order - 1], rys.at[order - 1], ryr.at[order - 1], me.at_y(order)))
-
+            ship(1)
+
+    ring_tick(me, go, 9, wall, ws, wr)
+    ring_tick(me, go, 10, wall, ws, wr)
     items = [opart[me.y].reshape(nrow, PW)]
     for d in (2, 1, 3):
-        blk = ry.at[d - 1]
-        rdma(blk, blk, rys.at[d - 1], ryr.at[d - 1], me.at_y(d)).wait_recv()
+        for part, at in ((0, pl.ds(0, GW // 2)), (1, pl.ds(GW // 2, PW - GW // 2))):
+            blk = ry.at[d - 1, :, :, at]
+            rdma(blk, blk, rys.at[part, d - 1], ryr.at[part, d - 1], me.at_y(d)).wait_recv()
         items.append(ry[d - 1].reshape(nrow, PW))
     mg[...] = join_partials(items).reshape(NZ, ROWS, PW)
     for d in (4, 3, 5, 2, 6, 1, 7):
         go(rdma(mg.at[me.zz(d)], rz.at[d - 1], rzs.at[d - 1], rzr.at[d - 1], me.at_z(d)))
+    ring_tick(me, go, 11, wall, ws, wr)
     items = [mg[me.z]]
     for d in range(1, NZ):
         blk = rz.at[d - 1]
         rdma(blk, blk, rzs.at[d - 1], rzr.at[d - 1], me.at_z(d)).wait_recv()
         items.append(rz[d - 1])
     att = join_partials(items, final=True)
-
+    ring_tick(me, go, 12, wall, ws, wr)
+    ring_tick(me, go, 13, wall, ws, wr)
+
+    plane = [(dy, dv) for dv in (4, 3, 5, 2, 6, 1, 7, 0) for dy in (2, 1, 3, 0)][:-1]
     for j in range(NY):
         tin[0, j] = att[:, j * FEAT : (j + 1) * FEAT]
     aall[me.v, me.y] = tin[0, me.y]
-    for d in (2, 1, 3):
-        go(rdma(tin.at[0, me.yy(d)], aall.at[me.v, me.y], tss.at[d - 1], trs.at[d - 1], me.at_y(d)))
-    for d in (2, 1, 3):
-        blk = aall.at[me.v, me.yy(-d)]
-        rdma(blk, blk, tss.at[d - 1], trs.at[d - 1], me.at_y(d)).wait_recv()
-    for d in (4, 3, 5, 2, 6, 1, 7):
-        blk = aall.at[me.v]
-        go(rdma(blk, blk, avs.at[d - 1], avr.at[d - 1], me.at_v(d)))
+    for dy, dv in plane:
+        dev = (me.z * NY + me.yy(dy), lax.rem(me.v + dv, NV))
+        go(rdma(tin.at[0, me.yy(dy)], aall.at[me.v, me.y], avs.at[dv, dy], avr.at[dv, dy], dev))
+    tok = NY * ROWS
+    for dy, dv in reversed(plane):
+        blk = aall.at[lax.rem(me.v - dv + NV, NV), me.yy(-dy)]
+        rdma(blk, blk, avs.at[dv, dy], avr.at[dv, dy], me.at_y(1)).wait_recv()
     ring_wait(me, wall, ws, wr)
-    tok = NY * ROWS
-    proj = jnp.dot(aall[me.v].reshape(tok, FEAT), wall[me.v], preferred_element_type=F32)
-    for d in (1, 7, 2, 6, 3, 5, 4):
-        src = lax.rem(me.v - d + NV, NV)
-        blk = aall.at[src]
-        rdma(blk, blk, avs.at[d - 1], avr.at[d - 1], me.at_v(1)).wait_recv()
-        proj = proj + jnp.dot(aall[src].reshape(tok, FEAT), wall[src], preferred_element_type=F32)
+    lhs = jnp.concatenate([aall[g].reshape(tok, FEAT) for g in range(NV)], axis=1)
+    proj = jnp.dot(lhs, wall[...].reshape(NV * FEAT, GW), preferred_element_type=F32)
     ppart[...] = proj.astype(BF).reshape(NY, ROWS, GW)
     for d in (2, 1, 3):
         go(rdma(ppart.at[me.yy(d)], rp.at[d - 1], ps_.at[d - 1], pr_.at[d - 1], me.at_y(d)))
+    for cp in later[1:3]:
+        cp.wait()
     total = res_ref[...].astype(F32) + ppart[me.y].astype(F32)
     for d in (1, 3, 2):
         blk = rp.at[d - 1]
@@ -323,54 +358,61 @@
     mean = jnp.sum(sq[...], axis=0)[:, :1] * (1.0 / D)
     nall[me.y, me.z] = (wide * lax.rsqrt(mean + EPSILON) * gain_ref[...]).astype(BF)
     gather_start(me, go, nall, hz, hzr)
-    gather_seq(me, go, nall, hz, hzr, hy, hyr)
-    own_hw.wait()
-    gather_wait(me, nall, hy, hyr)
+    for cp in later[:1] + later[3:]:
+        cp.wait()
 
     shift = (2, 1, 3, 0)
-
-    def rows_of(core):
-        blocks = []
-        for d in shift:
-            for y in range(NY):
-                blocks.append(nall[y, me.xx(d) * 2 + core])
-        return jnp.concatenate(blocks, axis=0)
-
-    sib = me.at_x(0, 1 - me.c)
-    lhs = rows_of(1 - me.c)
-    for n in range(NT):
-        at = pl.ds(n * TILE, TILE)
-        osend[n] = (
-            jnp.dot(lhs, hw_ref[:, at], preferred_element_type=F32).astype(BF).reshape(NX, tok, TILE)
-        )
-        go(rdma(osend.at[n], orecv.at[n], cs.at[n], cr.at[n], sib))
-    lhs = rows_of(me.c)
-    for n in range(NT):
-        at = pl.ds(n * TILE, TILE)
-        mine = jnp.dot(lhs, hw_ref[:, at], preferred_element_type=F32).reshape(NX, tok, TILE)
-        rdma(orecv.at[n], orecv.at[n], cs.at[n], cr.at[n], sib).wait_recv()
-        mine = mine + orecv[n].astype(F32)
-        own[n] = mine[3]
-        sx[n] = mine[:3].astype(BF)
+    for d in (0, 1, 7, 2, 6, 3, 5, 4):
+        gather_pass(me, go, nall, me.zz(d), d == 0, hz, hzr, hy, hyr)
+
+    def multiply(o):
+        yy = me.yy(-o)
+        if o:
+            for d in (0, 1, 7, 2, 6, 3, 5, 4):
+                gather_wait(me, nall, o, me.zz(d), hy, hyr)
+        blocks = [nall[yy, me.xx(d) * 2 + core] for core in (1 - me.c, me.c) for d in shift]
+        lhs = jnp.concatenate(blocks, axis=0)
+        for n in range(NT):
+            at = pl.ds(n * TILE, TILE)
+            both = jnp.dot(lhs, hw_ref[:, at], preferred_element_type=F32)
+            osend[o, :, :, at] = both[:tok].astype(BF).reshape(NX, ROWS, TILE)
+            own[o, :, :, at] = both[tok:].reshape(NX, ROWS, TILE)
+        go(rdma(osend.at[o], orecv.at[o], cs.at[o], cr.at[o], me.at_x(0, 1 - me.c)))
+
+    def pass_on(o):
+        rdma(orecv.at[o], orecv.at[o], cs.at[o], cr.at[o], me.at_x(0, 1 - me.c)).wait_recv()
         for i, d in enumerate(shift[:3]):
-            go(rdma(sx.at[n, i], x2.at[n, i], xs.at[n, i], xr.at[n, i], me.at_x(d, me.c)))
+            sx[o, i] = (own[o, i] + orecv[o, i].astype(F32)).astype(BF)
+            go(rdma(sx.at[o, i], x2.at[o, i], xs.at[o, i], xr.at[o, i], me.at_x(d, me.c)))
+        at = pl.ds(pl.multiple_of(me.yy(-o) * ROWS, ROWS), ROWS)
+        final[at] = own[o, 3] + orecv[o, 3].astype(F32)
+
+    turns = (0, 1, 3, 2)
+    multiply(turns[0])
+    for before, o in zip(turns, turns[1:]):
+        pass_on(before)
+        multiply(o)
+    pass_on(turns[3])
 
     tgt = jnp.concatenate([tgt_ref[...], jnp.zeros((1, 128 - tok), jnp.int32)], axis=1)
     tgt = jnp.broadcast_to(tgt.astype(F32), (128, 128))
     tgt = jnp.transpose(tgt)[:tok, :1].astype(jnp.int32) - me.s * VOC
     peak = None
+    for o in turns:
+        at = pl.ds(pl.multiple_of(me.yy(-o) * ROWS, ROWS), ROWS)
+        lg = final[at]
+        for i in range(3):
+            rdma(x2.at[o, i], x2.at[o, i], xs.at[o, i], xr.at[o, i], me.at_x(1, me.c)).wait_recv()
+            lg = lg + x2[o, i].astype(F32)
+        final[at] = lg
     for n in range(NT):
-        lg = own[n]
-        for i, d in enumerate(shift[:3]):
-            blk = x2.at[n, i]
-            rdma(blk, blk, xs.at[n, i], xr.at[n, i], me.at_x(d, me.c)).wait_recv()
-            lg = lg + x2[n, i].astype(F32)
-        own[n] = lg
+        at = pl.ds(n * TILE, TILE)
+        lg = final[:, at]
         top = jnp.max(lg, axis=1, keepdims=True)
         peak = top if peak is None else jnp.maximum(peak, top)
     total = picked = None
     for n in range(NT):
-        lg = own[n]
+        lg = final[:, pl.ds(n * TILE, TILE)]
         a = jnp.sum(jnp.exp(lg - peak), axis=1, keepdims=True)
         b = jnp.sum(jnp.where(lanes((tok, TILE)) + n * TILE == tgt, lg, 0.0), axis=1, keepdims=True)
         total = a if total is None else total + a
@@ -425,8 +467,7 @@
             jax.ShapeDtypeStruct((ROWS, GW), BF),
             jax.ShapeDtypeStruct((1, tok), F32),
         ),
-        in_specs=[any_, vm(), vm(), any_, any_, pl.BlockSpec(memory_space=pltpu.SMEM)]
-        + [any_, vm(), vm(), any_, vm()],
+        in_specs=[any_] * 5 + [pl.BlockSpec(memory_space=pltpu.SMEM)] + [any_] * 5,
         out_specs=(vm(), vm()),
         scratch_shapes=[
             pltpu.VMEM((NY, NZ, ROWS, GW), BF),
@@ -441,27 +482,31 @@
             pltpu.VMEM((NZ - 1, ROWS, PW), BF),
             pltpu.VMEM((NZ, FEAT, GW), BF),
             pltpu.VMEM((GW, VOC), BF),
+            pltpu.VMEM((ROWS, GW), BF),
+            pltpu.VMEM((1, GW), F32),
+            pltpu.VMEM((1, tok), jnp.int32),
             pltpu.VMEM((1, NY, ROWS, FEAT), BF),
             pltpu.VMEM((NV, NY, ROWS, FEAT), BF),
             pltpu.VMEM((NY, ROWS, GW), BF),
             pltpu.VMEM((NY - 1, ROWS, GW), BF),
             pltpu.VMEM((NV, ROWS, 128), F32),
             pltpu.VMEM((NY, NZ, ROWS, GW), BF),
-            pltpu.VMEM((NT, NX, tok, TILE), BF),
-            pltpu.VMEM((NT, NX, tok, TILE), BF),
-            pltpu.VMEM((NT, tok, TILE), F32),
-            pltpu.VMEM((NT, NX - 1, tok, TILE), BF),
-            pltpu.VMEM((NT, NX - 1, tok, TILE), BF),
+            pltpu.VMEM((NY, NX, ROWS, VOC), BF),
+            pltpu.VMEM((NY, NX, ROWS, VOC), BF),
+            pltpu.VMEM((NY, NX, ROWS, VOC), F32),
+            pltpu.VMEM((tok, VOC), F32),
+            pltpu.VMEM((NY, NX - 1, ROWS, VOC), BF),
+            pltpu.VMEM((NY, NX - 1, ROWS, VOC), BF),
             pltpu.VMEM((NY, 8, 128), F32),
             pltpu.VMEM((NZ, 8, 128), F32),
-            dma(3), dma(2, NV - 1), dma(NV), dma(NV),
-            dma(NZ - 1), dma(NZ - 1), dma(NY - 1, NZ), dma(NY - 1, NZ),
-            dma(2, NZ // 2), dma(2, NZ // 2),
-            dma(NY - 1), dma(NY - 1), dma(NZ - 1), dma(NZ - 1),
+            dma(8), dma(2, NV - 1), dma(NV), dma(NV),
+            dma(NZ - 1), dma(NZ), dma(NY - 1, NZ), dma(NY - 1, NZ),
+            dma(2, len(TICKS)), dma(2, NZ // 2 * PIECES),
+            dma(2, NY - 1), dma(2, NY - 1), dma(NZ - 1), dma(NZ - 1),
+            dma(NV, NY), dma(NV, NY),
             dma(NY - 1), dma(NY - 1), dma(NV - 1), dma(NV - 1),
-            dma(NY - 1), dma(NY - 1), dma(NV - 1), dma(NV - 1),
-            dma(NZ - 1), dma(NZ - 1), dma(NY - 1, NZ), dma(NY - 1, NZ),
-            dma(NT), dma(NT), dma(NT, NX - 1), dma(NT, NX - 1),
+            dma(NZ - 1), dma(NZ), dma(NY - 1, NZ), dma(NY - 1, NZ),
+            dma(NY), dma(NY), dma(NY, NX - 1), dma(NY, NX - 1),
             dma(NY - 1), dma(NY - 1), dma(NZ - 1), dma(NZ - 1),
         ],
         compiler_params=params(0),

time: 134 us -> 115 us (0.86)
  Pallas kernels: 130 us -> 111 us
    pallas_call x1, Pallas kernels: 130 us -> 111 us  [shards(): pl.pallas_call(kernel, out_shape=(jax.ShapeDtypeStruct((ROWS, GW), BF), j...]
where the time goes in v3:
time: 115 us
  Pallas kernels  111 us (97%)
  local copies, waits for them, and re-layouts  2.55 us (2%)
  between operations  1.29 us (1%)
    pallas_call x1, Pallas kernels, shards(): pl.pallas_call(kernel, out_shape=(jax.ShapeDtypeStruct((ROWS, GW), BF), j...  111 us
    unnamed x2, local copies, waits for them, and re-layouts  2.55 us

profile of v3, /device:TPU:8, one launch (start us, length us, event | category | flops | bytes accessed | tf_op | source)
XLA Modules:
  0.0 115.0 jit_solution(8140166467979617418)
XLA Ops:
  1.3 111.1 %layer.1 = (bf16[16,1024]{1,0:T(8,128)(2,1)}, f32[1,64]{1,0:T(1,128)}) custom-call(bf16[16,8192]{1,0:T(8,128)(2,1)} %q_ref.1, bf16[16,1024]{1,0:T(8,128)(2,1)} %sk_ref.1, bf16[16,1024]{1,0:T(8,128)(2,1)} %sv_ref.1, bf16[256,1024]{1,0:T(8,128)(2,1)} %ck_ref.1, bf16[256,1024]{1,0:T(8,128)(2,1)} %cv_ref.1, s32[1]{0:T(128)S(6)} %copy.15.start_ref, ...), custom_call_target="tpu_custom_call" | custom-call | tf_op jit(solution)/shard_map/layer/pallas_call | solution.py:464
  112.4 1.4 %copy.16 = bf16[16,1024]{1,0:T(8,128)(2,1)} copy(bf16[16,1024]{1,0:T(8,128)(2,1)} %get-tuple-element.8) | data formatting | bytes 65536
  113.8 1.2 %copy.17 = f32[64]{0:T(128)} copy(f32[64]{0:T(128)} %bitcast.5) | data formatting | bytes 512

commit v4 on v3

--- a/solution.py
+++ b/solution.py
@@ -167,9 +167,9 @@
 def kernel(
     q_ref, sk_ref, sv_ref, ck_ref, cv_ref, start_ref, w_ref, res_hbm, gain_hbm, hw_hbm, tgt_hbm,
     hid_ref, out_ref,
-    qall, kbuf, vbuf, vext, bias, lse_buf, opart, ry, mg, rz, wall, hw_ref, res_ref, gain_ref, tgt_ref, tin, aall, ppart, rp, sq, nall,
+    qall, kbuf, vbuf, vext, bias, lse_buf, opart, ry, mg, rz, wall, hw_ref, res_ref, gain_ref, tgt_ref, tin, aall, ppart, rp, sq, nall, scy, scz, scale_of,
     osend, orecv, own, final, sx, x2, sty, stz,
-    loc, kvs, kr, vr, gz, gzr, gy, gyr, ws, wr, rys, ryr, rzs, rzr, avs, avr, ps_, pr_, sqs, sqr,
+    loc, kvs, kr, vr, gz, gzr, gy, gyr, ws, wr, rys, ryr, rzs, rzr, avs, avr, ps_, pr_, sqs, sqr, scs, scr, sczs, sczr,
     hz, hzr, hy, hyr, cs, cr, xs, xr, yss, yrs, zss, zrs,
 ):
     me = Place()
@@ -348,29 +348,53 @@
     hidden = total.astype(BF)
     hid_ref[...] = hidden
 
+    nall[me.y, me.z] = hidden
+    gather_start(me, go, nall, hz, hzr)
     wide = hidden.astype(F32)
     sq[me.v] = jnp.broadcast_to(jnp.sum(wide * wide, axis=1, keepdims=True), (ROWS, 128))
     for d in (4, 3, 5, 2, 6, 1, 7):
         go(rdma(sq.at[me.v], sq.at[me.v], sqs.at[d - 1], sqr.at[d - 1], me.at_v(d)))
+    gather_pass(me, go, nall, me.z, True, hz, hzr, hy, hyr)
     for d in range(1, NV):
         blk = sq.at[lax.rem(me.v - d + NV, NV)]
         rdma(blk, blk, sqs.at[d - 1], sqr.at[d - 1], me.at_v(1)).wait_recv()
-    mean = jnp.sum(sq[...], axis=0)[:, :1] * (1.0 / D)
-    nall[me.y, me.z] = (wide * lax.rsqrt(mean + EPSILON) * gain_ref[...]).astype(BF)
-    gather_start(me, go, nall, hz, hzr)
+    mean = jnp.sum(sq[...], axis=0) * (1.0 / D)
+    spread = jnp.transpose(jnp.concatenate([lax.rsqrt(mean + EPSILON)] * (128 // ROWS), axis=0))[:8]
+    scy[0] = jnp.where(lax.div(lanes((8, 128)), ROWS) == me.y, spread, 0.0)
+    for d in (2, 1, 3):
+        go(rdma(scy.at[0], scy.at[d], scs.at[d - 1], scr.at[d - 1], me.at_y(d)))
+    for d in (1, 7):
+        gather_pass(me, go, nall, me.zz(d), False, hz, hzr, hy, hyr)
+    for d in (2, 1, 3):
+        rdma(scy.at[d], scy.at[d], scs.at[d - 1], scr.at[d - 1], me.at_y(d)).wait_recv()
+    scz[me.z] = scy[0] + scy[1] + scy[2] + scy[3]
+    for d in (4, 3, 5, 2, 6, 1, 7):
+        go(rdma(scz.at[me.z], scz.at[me.z], sczs.at[d - 1], sczr.at[me.z], me.at_z(d)))
+    for d in (2, 6, 3, 5, 4):
+        gather_pass(me, go, nall, me.zz(d), False, hz, hzr, hy, hyr)
+    for d in range(1, NZ):
+        blk = scz.at[me.zz(d)]
+        rdma(blk, blk, sczs.at[0], sczr.at[me.zz(d)], me.at_z(1)).wait_recv()
+    turned = [scz[i, 0:1] for i in range(NZ)] + [jnp.zeros((128 - NZ, 128), F32)]
+    scale_of[...] = jnp.transpose(jnp.concatenate(turned, axis=0))
     for cp in later[:1] + later[3:]:
         cp.wait()
 
     shift = (2, 1, 3, 0)
-    for d in (0, 1, 7, 2, 6, 3, 5, 4):
-        gather_pass(me, go, nall, me.zz(d), d == 0, hz, hzr, hy, hyr)
 
     def multiply(o):
         yy = me.yy(-o)
         if o:
             for d in (0, 1, 7, 2, 6, 3, 5, 4):
                 gather_wait(me, nall, o, me.zz(d), hy, hyr)
-        blocks = [nall[yy, me.xx(d) * 2 + core] for core in (1 - me.c, me.c) for d in shift]
+        scales = scale_of[pl.ds(pl.multiple_of(yy * ROWS, ROWS), ROWS)]
+        blocks = []
+        for core in (1 - me.c, me.c):
+            for d in shift:
+                zz = me.xx(d) * 2 + core
+                rs = jnp.where(lanes((ROWS, 128)) == zz, scales, 0.0)
+                rs = jnp.sum(rs, axis=1, keepdims=True)
+                blocks.append((nall[yy, zz].astype(F32) * rs * gain_ref[...]).astype(BF))
         lhs = jnp.concatenate(blocks, axis=0)
         for n in range(NT):
             at = pl.ds(n * TILE, TILE)
@@ -442,6 +466,11 @@
     out_ref[...] = (pick - (top + jnp.log(tot)))[:, :tok]
     for cp in sends:
         cp.wait_send()
+
+
+def hand_over(hid_ref, logprob_ref, hid_out, logprob_out):
+    hid_out[...] = hid_ref[...]
+    logprob_out[...] = logprob_ref[0, :]
 
 
 def vm():
@@ -491,6 +520,9 @@
             pltpu.VMEM((NY - 1, ROWS, GW), BF),
             pltpu.VMEM((NV, ROWS, 128), F32),
             pltpu.VMEM((NY, NZ, ROWS, GW), BF),
+            pltpu.VMEM((NY, 8, 128), F32),
+            pltpu.VMEM((NZ, 8, 128), F32),
+            pltpu.VMEM((128, 128), F32),
             pltpu.VMEM((NY, NX, ROWS, VOC), BF),
             pltpu.VMEM((NY, NX, ROWS, VOC), BF),
             pltpu.VMEM((NY, NX, ROWS, VOC), F32),
@@ -505,6 +537,7 @@
             dma(2, NY - 1), dma(2, NY - 1), dma(NZ - 1), dma(NZ - 1),
             dma(NV, NY), dma(NV, NY),
             dma(NY - 1), dma(NY - 1), dma(NV - 1), dma(NV - 1),
+            dma(NY - 1), dma(NY - 1), dma(NZ - 1), dma(NZ),
             dma(NZ - 1), dma(NZ), dma(NY - 1, NZ), dma(NY - 1, NZ),
             dma(NY), dma(NY), dma(NY, NX - 1), dma(NY, NX - 1),
             dma(NY - 1), dma(NY - 1), dma(NZ - 1), dma(NZ - 1),
@@ -512,7 +545,13 @@
         compiler_params=params(0),
         name="layer",
     )(q, sk, sv, ck, cv, start, w, res, gain.reshape(1, GW), hw, tgt.reshape(1, tok))
-    return hidden, logprobs.reshape(tok)
+    return pl.pallas_call(
+        hand_over,
+        out_shape=(jax.ShapeDtypeStruct((ROWS, GW), BF), jax.ShapeDtypeStruct((tok,), F32)),
+        in_specs=[vm(), vm()],
+        out_specs=(vm(), vm()),
+        name="results",
+    )(hidden, logprobs)
 
 
 def solution(mesh):

time: 115 us -> 112 us (0.974)
  local copies, waits for them, and re-layouts: 2.55 us -> 0 us
    unnamed x2 -> x0, local copies, waits for them, and re-layouts: 2.55 us -> none
    pallas_call x1, Pallas kernels: 111 us -> 109 us  [shards(): pl.pallas_call(kernel, out_shape=(jax.ShapeDtypeStruct((ROWS, GW), BF), j...]
    pallas_call x0 -> x1, Pallas kernels: none -> 1.38 us  [shards(): pl.pallas_call(hand_over, out_shape=(jax.ShapeDtypeStruct((ROWS, GW), BF)...]
where the time goes in v4:
time: 112 us
  Pallas kernels  111 us (99%)
  between operations  1.29 us (1%)
    pallas_call x1, Pallas kernels, shards(): pl.pallas_call(kernel, out_shape=(jax.ShapeDtypeStruct((ROWS, GW), BF), j...  109 us

profile of v4, /device:TPU:8, one launch (start us, length us, event | category | flops | bytes accessed | tf_op | source)
XLA Modules:
  0.0 111.9 jit_solution(4892079078576129695)
XLA Ops:
  1.3 109.2 %layer.1 = (bf16[16,1024]{1,0:T(8,128)(2,1)}, f32[1,64]{1,0:T(1,128)}) custom-call(bf16[16,8192]{1,0:T(8,128)(2,1)} %q_ref.1, bf16[16,1024]{1,0:T(8,128)(2,1)} %sk_ref.1, bf16[16,1024]{1,0:T(8,128)(2,1)} %sv_ref.1, bf16[256,1024]{1,0:T(8,128)(2,1)} %ck_ref.1, bf16[256,1024]{1,0:T(8,128)(2,1)} %cv_ref.1, s32[1]{0:T(128)S(6)} %copy.13.start_ref, ...), custom_call_target="tpu_custom_call" | custom-call | tf_op jit(solution)/shard_map/layer/pallas_call | solution.py:493
  110.5 1.4 %results.1 = (bf16[16,1024]{1,0:T(8,128)(2,1)}, f32[64]{0:T(128)}) custom-call(bf16[16,1024]{1,0:T(8,128)(2,1)} %get-tuple-element.4.hid_ref, f32[1,64]{1,0:T(1,128)} %get-tuple-element.5.logprob_ref), custom_call_target="tpu_custom_call" | custom-call | tf_op jit(solution)/shard_map/results/pallas_call | solution.py:548

commit v5 on v4

--- a/solution.py
+++ b/solution.py
@@ -77,11 +77,11 @@
         go(rdma(own, own, zs.at[d - 1], zr.at[me.z], me.at_z(d)))
 
 
-def gather_pass(me, go, buf, src, own, zs, zr, ys, yr):
+def gather_pass(me, go, buf, src, own, zs, zr, ys, yr, order=(2, 1, 3)):
     blk = buf.at[me.y, src]
     if not own:
         rdma(blk, blk, zs.at[0], zr.at[src], me.at_z(1)).wait_recv()
-    for e in (2, 1, 3):
+    for e in order:
         go(rdma(blk, blk, ys.at[e - 1, src], yr.at[e - 1, src], me.at_y(e)))
 
 
@@ -168,7 +168,7 @@
     q_ref, sk_ref, sv_ref, ck_ref, cv_ref, start_ref, w_ref, res_hbm, gain_hbm, hw_hbm, tgt_hbm,
     hid_ref, out_ref,
     qall, kbuf, vbuf, vext, bias, lse_buf, opart, ry, mg, rz, wall, hw_ref, res_ref, gain_ref, tgt_ref, tin, aall, ppart, rp, sq, nall, scy, scz, scale_of,
-    osend, orecv, own, final, sx, x2, sty, stz,
+    osend, orecv, own, final, sx, x2, tgt_of, st_of, sty, stz,
     loc, kvs, kr, vr, gz, gzr, gy, gyr, ws, wr, rys, ryr, rzs, rzr, avs, avr, ps_, pr_, sqs, sqr, scs, scr, sczs, sczr,
     hz, hzr, hy, hyr, cs, cr, xs, xr, yss, yrs, zss, zrs,
 ):
@@ -354,7 +354,7 @@
     sq[me.v] = jnp.broadcast_to(jnp.sum(wide * wide, axis=1, keepdims=True), (ROWS, 128))
     for d in (4, 3, 5, 2, 6, 1, 7):
         go(rdma(sq.at[me.v], sq.at[me.v], sqs.at[d - 1], sqr.at[d - 1], me.at_v(d)))
-    gather_pass(me, go, nall, me.z, True, hz, hzr, hy, hyr)
+    gather_pass(me, go, nall, me.z, True, hz, hzr, hy, hyr, (1, 3, 2))
     for d in range(1, NV):
         blk = sq.at[lax.rem(me.v - d + NV, NV)]
         rdma(blk, blk, sqs.at[d - 1], sqr.at[d - 1], me.at_v(1)).wait_recv()
@@ -364,14 +364,14 @@
     for d in (2, 1, 3):
         go(rdma(scy.at[0], scy.at[d], scs.at[d - 1], scr.at[d - 1], me.at_y(d)))
     for d in (1, 7):
-        gather_pass(me, go, nall, me.zz(d), False, hz, hzr, hy, hyr)
+        gather_pass(me, go, nall, me.zz(d), False, hz, hzr, hy, hyr, (1, 3, 2))
     for d in (2, 1, 3):
         rdma(scy.at[d], scy.at[d], scs.at[d - 1], scr.at[d - 1], me.at_y(d)).wait_recv()
     scz[me.z] = scy[0] + scy[1] + scy[2] + scy[3]
     for d in (4, 3, 5, 2, 6, 1, 7):
         go(rdma(scz.at[me.z], scz.at[me.z], sczs.at[d - 1], sczr.at[me.z], me.at_z(d)))
     for d in (2, 6, 3, 5, 4):
-        gather_pass(me, go, nall, me.zz(d), False, hz, hzr, hy, hyr)
+        gather_pass(me, go, nall, me.zz(d), False, hz, hzr, hy, hyr, (1, 3, 2))
     for d in range(1, NZ):
         blk = scz.at[me.zz(d)]
         rdma(blk, blk, sczs.at[0], sczr.at[me.zz(d)], me.at_z(1)).wait_recv()
@@ -411,6 +411,10 @@
         at = pl.ds(pl.multiple_of(me.yy(-o) * ROWS, ROWS), ROWS)
         final[at] = own[o, 3] + orecv[o, 3].astype(F32)
 
+    tgt = jnp.concatenate([tgt_ref[...], jnp.zeros((1, 128 - tok), jnp.int32)], axis=1)
+    tgt = jnp.transpose(jnp.broadcast_to(tgt.astype(F32), (128, 128)))
+    tgt_of[...] = tgt[:tok].astype(jnp.int32) - me.s * VOC
+
     turns = (0, 1, 3, 2)
     multiply(turns[0])
     for before, o in zip(turns, turns[1:]):
@@ -418,32 +422,19 @@
         multiply(o)
     pass_on(turns[3])
 
-    tgt = jnp.concatenate([tgt_ref[...], jnp.zeros((1, 128 - tok), jnp.int32)], axis=1)
-    tgt = jnp.broadcast_to(tgt.astype(F32), (128, 128))
-    tgt = jnp.transpose(tgt)[:tok, :1].astype(jnp.int32) - me.s * VOC
-    peak = None
+    lane = lanes((ROWS, 128))
     for o in turns:
         at = pl.ds(pl.multiple_of(me.yy(-o) * ROWS, ROWS), ROWS)
         lg = final[at]
         for i in range(3):
             rdma(x2.at[o, i], x2.at[o, i], xs.at[o, i], xr.at[o, i], me.at_x(1, me.c)).wait_recv()
             lg = lg + x2[o, i].astype(F32)
-        final[at] = lg
-    for n in range(NT):
-        at = pl.ds(n * TILE, TILE)
-        lg = final[:, at]
-        top = jnp.max(lg, axis=1, keepdims=True)
-        peak = top if peak is None else jnp.maximum(peak, top)
-    total = picked = None
-    for n in range(NT):
-        lg = final[:, pl.ds(n * TILE, TILE)]
-        a = jnp.sum(jnp.exp(lg - peak), axis=1, keepdims=True)
-        b = jnp.sum(jnp.where(lanes((tok, TILE)) + n * TILE == tgt, lg, 0.0), axis=1, keepdims=True)
-        total = a if total is None else total + a
-        picked = b if picked is None else picked + b
-    lane = lanes((tok, 128))
-    st = jnp.where(lane == 0, peak, jnp.where(lane == 1, total, picked))
-    st = jnp.concatenate([st, jnp.zeros((128 - tok, 128), F32)], axis=0)
+        peak = jnp.max(lg, axis=1, keepdims=True)
+        total = jnp.sum(jnp.exp(lg - peak), axis=1, keepdims=True)
+        hit = lanes((ROWS, VOC)) == tgt_of[at][:, :1]
+        picked = jnp.sum(jnp.where(hit, lg, 0.0), axis=1, keepdims=True)
+        st_of[at] = jnp.where(lane == 0, peak, jnp.where(lane == 1, total, picked))
+    st = jnp.concatenate([st_of[...], jnp.zeros((128 - tok, 128), F32)], axis=0)
     sty[0] = jnp.transpose(st)[:8]
 
     def joined(buf, count):
@@ -529,6 +520,8 @@
             pltpu.VMEM((tok, VOC), F32),
             pltpu.VMEM((NY, NX - 1, ROWS, VOC), BF),
             pltpu.VMEM((NY, NX - 1, ROWS, VOC), BF),
+            pltpu.VMEM((tok, 128), jnp.int32),
+            pltpu.VMEM((tok, 128), F32),
             pltpu.VMEM((NY, 8, 128), F32),
             pltpu.VMEM((NZ, 8, 128), F32),
             dma(8), dma(2, NV - 1), dma(NV), dma(NV),

time: 112 us -> 111 us (level)
  no operation moved by 1% of the time
where the time goes in v5:
time: 111 us
  Pallas kernels  110 us (99%)
  between operations  1.29 us (1%)
    pallas_call x1, Pallas kernels, shards(): pl.pallas_call(kernel, out_shape=(jax.ShapeDtypeStruct((ROWS, GW), BF), j...  108 us

profile of v5, /device:TPU:8, one launch (start us, length us, event | category | flops | bytes accessed | tf_op | source)
XLA Modules:
  0.0 111.0 jit_solution(17970627346066331359)
XLA Ops:
  1.3 108.4 %layer.1 = (bf16[16,1024]{1,0:T(8,128)(2,1)}, f32[1,64]{1,0:T(1,128)}) custom-call(bf16[16,8192]{1,0:T(8,128)(2,1)} %q_ref.1, bf16[16,1024]{1,0:T(8,128)(2,1)} %sk_ref.1, bf16[16,1024]{1,0:T(8,128)(2,1)} %sv_ref.1, bf16[256,1024]{1,0:T(8,128)(2,1)} %ck_ref.1, bf16[256,1024]{1,0:T(8,128)(2,1)} %cv_ref.1, s32[1]{0:T(128)S(6)} %copy.13.start_ref, ...), custom_call_target="tpu_custom_call" | custom-call | tf_op jit(solution)/shard_map/layer/pallas_call | solution.py:484
  109.7 1.4 %results.1 = (bf16[16,1024]{1,0:T(8,128)(2,1)}, f32[64]{0:T(128)}) custom-call(bf16[16,1024]{1,0:T(8,128)(2,1)} %get-tuple-element.4.hid_ref, f32[1,64]{1,0:T(1,128)} %get-tuple-element.5.logprob_ref), custom_call_target="tpu_custom_call" | custom-call | tf_op jit(solution)/shard_map/results/pallas_call | solution.py:541
